TPU v7x, 128 devices: a whole 4x4x4 slice. The times are simulated.
128 devices in a mesh: row: 16 (over x, y_lo, core), col: 8 (over z, y_hi).
Axes of the slice: x: 4, y: 4 (y_hi: 2, y_lo: 2; y = y_hi * 2 + y_lo), z: 4, core: 2. Of those that a mesh axis runs over, the one named last changes fastest.
Arguments:
- inputs: bfloat16 [768, 12288], P('row', 'col'), may hold values from -6 to 6
- first_values: bfloat16 [96, 96, 128, 128], P('col', 'row'), may hold values from -0.109375 to 0.109375
- first_blocks: int32 [96, 96], P('col', 'row'), may hold values from 0 to 383, as said below
- second_values: bfloat16 [384, 24, 128, 128], P('row', 'col'), may hold values from -0.0546875 to 0.0546875
- second_blocks: int32 [384, 24], P('row', 'col'), may hold values from 0 to 95, as said below
- cotangent: bfloat16 [768, 12288], P('row', 'col'), may hold values from -6 to 6
Outputs:
- outputs: bfloat16 [768, 12288], P('row', 'col')
- input_grad: bfloat16 [768, 12288], P('row', 'col')
- first_grad: bfloat16 [96, 96, 128, 128], P('col', 'row')
- second_grad: bfloat16 [384, 24, 128, 128], P('row', 'col')
Inputs may be any that keep to these rules, and one draw needn't show every extreme that they name: `first_blocks`: in block row i, slots g * 6 to (g + 1) * 6 - 1 name 6 different column blocks in increasing order, all within 4 * g * 6 to 4 * (g + 1) * 6 - 1. `second_blocks`: in block row j, slots g * 3 to (g + 1) * 3 - 1 name 3 different column blocks in increasing order, all within 4 * g * 3 to 4 * (g + 1) * 3 - 1.
All inputs are finite; a program needn't handle non-finite values.
Results may differ from a plain program's by a relative error of at most 0.0049.
Values may be sent and summed in bfloat16 or wider, within the bound.
A program may use at most 192 MiB of HBM per device.

v0:
```python
import jax
import jax.numpy as jnp
from jax import lax
from jax.sharding import PartitionSpec as P

gelu_scale = 0.7978845608028654
gelu_cubic = 0.044715


def gelu_pair(pre_act):
    inner_arg = gelu_scale * (pre_act + gelu_cubic * pre_act * pre_act * pre_act)
    tanh_value = jnp.tanh(inner_arg)
    activated = 0.5 * pre_act * (1.0 + tanh_value)
    derivative = 0.5 * (1.0 + tanh_value) + 0.5 * pre_act * (
        1.0 - tanh_value * tanh_value
    ) * gelu_scale * (1.0 + 3.0 * gelu_cubic * pre_act * pre_act)
    return (activated, derivative)


def row_height():
    return 256


def blocked(apply_block, operand):
    row_count = operand.shape[0]
    height = row_height()
    stacked = operand.reshape(row_count // height, height, operand.shape[1])
    result = lax.map(apply_block, stacked)
    return result.reshape(row_count, result.shape[-1])


def spread_rows(panels, values, local_index, out_blocks):
    flat_index = local_index.reshape(-1)

    def spread_one_block(row_block):
        height = row_block.shape[0]
        shaped = row_block.reshape(height, values.shape[0], values.shape[2])
        products = jnp.einsum("tik,isko->tiso", shaped, values, preferred_element_type=jnp.float32)
        products = products.reshape(height, values.shape[0] * values.shape[1], values.shape[3])
        placed = (
            jnp.zeros((height, out_blocks, values.shape[3]), jnp.float32)
            .at[:, flat_index, :]
            .add(products)
        )
        return placed.reshape(height, out_blocks * values.shape[3])

    return blocked(spread_one_block, panels)


def collect_rows(panels, values, local_index):

    def collect_one_block(row_block):
        height = row_block.shape[0]
        shaped = row_block.reshape(height, -1, values.shape[3])
        picked = jnp.take(shaped, local_index.reshape(-1), axis=1)
        picked = picked.reshape(height, values.shape[0], values.shape[1], values.shape[3])
        summed = jnp.einsum("tiso,isko->tik", picked, values, preferred_element_type=jnp.float32)
        return summed.reshape(height, values.shape[0] * values.shape[2])

    return blocked(collect_one_block, panels)


def block_grads(left, right, local_index, values):
    row_count = left.shape[0]
    height = row_height()
    count_blocks = row_count // height
    left_stack = left.reshape(count_blocks, height, values.shape[0], values.shape[2])
    right_stack = right.reshape(count_blocks, height, -1, values.shape[3])

    def accumulate(running, pair_rows):
        left_part, right_part = pair_rows
        picked = jnp.take(right_part, local_index.reshape(-1), axis=1)
        picked = picked.reshape(height, values.shape[0], values.shape[1], values.shape[3])
        update = jnp.einsum("tik,tiso->isko", left_part, picked, preferred_element_type=jnp.float32)
        return (running + update, None)

    initial = jnp.zeros(values.shape, jnp.float32)
    running, unused = lax.scan(accumulate, initial, (left_stack, right_stack))
    return running


def row_panel(local_rows):
    return lax.all_gather(local_rows, "row", axis=0, tiled=True)


def col_panel(local_rows):
    return lax.all_gather(local_rows, "col", axis=0, tiled=True)


def col_partial(term_fn, height):
    return lax.psum_scatter(
        term_fn(jnp.int32(0), height * lax.axis_size("col")), "col", scatter_dimension=0, tiled=True
    )


def row_partial(term_fn, height):
    return lax.psum_scatter(
        term_fn(jnp.int32(0), height * lax.axis_size("row")), "row", scatter_dimension=0, tiled=True
    )


def shards(inputs, first_values, first_blocks, second_values, second_blocks, cotangent):
    tile_blocks = first_values.shape[0]
    hidden_blocks = second_values.shape[0]
    local_first = first_blocks - lax.axis_index("row") * hidden_blocks
    local_second = second_blocks - lax.axis_index("col") * tile_blocks
    own_rows = inputs.shape[0]
    total_rows = own_rows * lax.axis_size("row")
    hidden_rows = total_rows // lax.axis_size("col")
    input_panel = row_panel(inputs)

    def first_term(first_row, height):
        return spread_rows(input_panel, first_values, local_first, hidden_blocks)

    pre_act = col_partial(first_term, hidden_rows)
    hidden_panel = col_panel(gelu_pair(pre_act)[0].astype(jnp.bfloat16))

    def second_term(first_row, height):
        return spread_rows(hidden_panel, second_values, local_second, tile_blocks)

    outputs = row_partial(second_term, own_rows).astype(jnp.bfloat16)
    grad_panel = row_panel(cotangent)

    def hidden_term(first_row, height):
        return collect_rows(grad_panel, second_values, local_second)

    hidden_grad = col_partial(hidden_term, hidden_rows)
    second_grad = block_grads(hidden_panel, grad_panel, local_second, second_values)
    pre_grad = (hidden_grad * gelu_pair(pre_act)[1]).astype(jnp.bfloat16)
    pre_panel = col_panel(pre_grad)

    def input_term(first_row, height):
        return collect_rows(pre_panel, first_values, local_first)

    input_grad = row_partial(input_term, own_rows).astype(jnp.bfloat16)
    first_grad = block_grads(input_panel, pre_panel, local_first, first_values)
    return (outputs, input_grad, first_grad.astype(jnp.bfloat16), second_grad.astype(jnp.bfloat16))


def solution(mesh):
    placed = (
        P("row", "col"),
        P("col", "row", None, None),
        P("col", "row"),
        P("row", "col", None, None),
        P("row", "col"),
        P("row", "col"),
    )
    return jax.shard_map(
        shards,
        mesh=mesh,
        in_specs=placed,
        out_specs=(
            P("row", "col"),
            P("row", "col"),
            P("col", "row", None, None),
            P("row", "col", None, None),
        ),
        check_vma=False,
    )
```

profile of v0, /device:TPU:0, one launch (start us, length us, event | category | flops | bytes accessed | tf_op | source)
XLA Modules:
  0.0 750.6 jit_solution(13523754431960236858)
XLA Ops:
  9.6 36.9 %all-gather.9.cloned.1.call-done = bf16[768,1536]{1,0:T(8,128)(2,1)} async-done(((bf16[48,1536]{1,0:T(8,128)(2,1)}), bf16[768,1536]{1,0:T(8,128)(2,1)}) %all-gather.9.cloned.1.call-update) | async-done | bytes 2359312 | tf_op jit(solution)/shard_map/all_gather | solution.py:83
  51.3 58.5 %while.68 = (s32[]{:T(128)}, f32[3,256,3072]{2,1,0:T(8,128)}, bf16[3,256,1536]{2,1,0:T(8,128)(2,1)}, s32[24,3]{1,0:T(8,128)}, bf16[24,3,128,128]{3,2,1,0:T(8,128)(2,1)}, /*index=5*/s32[72]{0:T(128)S(1)}, s32[]{:T(128)}) while((s32[]{:T(128)}, f32[3,256,3072]{2,1,0:T(8,128)}, bf16[3,256,1536]{2,1,0:T(8,128)(2,1)}, ...), condition=%wide.wide.region_9.11_spmd, body=%wide.wide.region_8.10_spmd.sunk | while | flops 606340736 | bytes 46405760 | solution.py:28
  115.5 91.8 %while.66 = (s32[]{:T(128)}, f32[3,256,3072]{2,1,0:T(8,128)}, s32[72]{0:T(128)S(1)}, bf16[3,256,1536]{2,1,0:T(8,128)(2,1)}, bf16[12,6,128,128]{3,2,1,0:T(8,128)(2,1)}, /*index=5*/s32[]{:T(128)}, f32[]{:T(128)}) while((s32[]{:T(128)}, f32[3,256,3072]{2,1,0:T(8,128)}, s32[72]{0:T(128)S(1)}, bf16[3,256,1536]{2,1,0:T(8,128)(2,1)}, ...), condition=%wide.region_2.3_spmd, body=%wide.region_0.2_spmd.sunk | while | flops 606339264 | bytes 66061748 | solution.py:28
  117.0 6.7 fusion.55
  124.0 15.2 %scatter_fusion = f32[256,24,128]{2,0,1:T(8,128)S(1)} fusion(f32[256,24,128]{2,0,1:T(8,128)S(1)} %broadcast.192, s32[72]{0:T(128)S(1)} %fusion.54, f32[72,256,128]{2,1,0:T(8,128)} %bitcast.190), kind=kCustom, calls=%fused_computation.4.clone.1 | custom fusion | flops 2359296 | bytes 28311840 | tf_op jit(solution)/shard_map/while/body/eval_jaxpr/scatter-add | solution.py:43
  147.6 7.0 fusion.55
  154.9 15.3 %scatter_fusion = f32[256,24,128]{2,0,1:T(8,128)S(1)} fusion(f32[256,24,128]{2,0,1:T(8,128)S(1)} %broadcast.192, s32[72]{0:T(128)S(1)} %fusion.54, f32[72,256,128]{2,1,0:T(8,128)} %bitcast.190), kind=kCustom, calls=%fused_computation.4.clone.1 | custom fusion | flops 2359296 | bytes 28311840 | tf_op jit(solution)/shard_map/while/body/eval_jaxpr/scatter-add | solution.py:43
  178.4 6.8 fusion.55
  185.5 15.1 %scatter_fusion = f32[256,24,128]{2,0,1:T(8,128)S(1)} fusion(f32[256,24,128]{2,0,1:T(8,128)S(1)} %broadcast.192, s32[72]{0:T(128)S(1)} %fusion.54, f32[72,256,128]{2,1,0:T(8,128)} %bitcast.190), kind=kCustom, calls=%fused_computation.4.clone.1 | custom fusion | flops 2359296 | bytes 28311840 | tf_op jit(solution)/shard_map/while/body/eval_jaxpr/scatter-add | solution.py:43
  207.4 27.8 %reduce-scatter.9.cloned.1.call-done = f32[96,3072]{1,0:T(8,128)} async-done(((f32[768,3072]{1,0:T(8,128)}), f32[96,3072]{1,0:T(8,128)}) %reduce-scatter.9.cloned.1.call-update) | async-done | bytes 1179664 | tf_op jit(solution)/shard_map/reduce_scatter | solution.py:91
  235.2 126.5 %reduce-scatter.5.cloned.1.call-done = f32[96,3072]{1,0:T(8,128)} async-done(((f32[768,3072]{1,0:T(8,128)}), f32[96,3072]{1,0:T(8,128)}) %reduce-scatter.5.cloned.1.call-update) | async-done | bytes 1179664 | tf_op jit(solution)/shard_map/reduce_scatter | solution.py:91
  366.1 73.1 %all-gather.11.cloned.1.call-done = bf16[768,3072]{1,0:T(8,128)(2,1)} async-done(((bf16[96,3072]{1,0:T(8,128)(2,1)}), bf16[768,3072]{1,0:T(8,128)(2,1)}) %all-gather.11.cloned.1.call-update) | async-done | bytes 4718608 | tf_op jit(solution)/shard_map/all_gather | solution.py:87
  441.8 50.0 %while.69 = (s32[]{:T(128)}, f32[3,256,1536]{2,1,0:T(8,128)}, bf16[3,256,3072]{2,1,0:T(8,128)(2,1)}, s32[12,6]{1,0:T(8,128)}, bf16[12,6,128,128]{3,2,1,0:T(8,128)(2,1)}, /*index=5*/s32[72]{0:T(128)S(1)}, s32[]{:T(128)}) while((s32[]{:T(128)}, f32[3,256,1536]{2,1,0:T(8,128)}, bf16[3,256,3072]{2,1,0:T(8,128)(2,1)}, ...), condition=%wide.wide.region_12.15_spmd, body=%wide.wide.region_11.14_spmd.sunk | while | flops 606340736 | bytes 43260032 | solution.py:28
  523.5 79.0 %while.67 = (s32[]{:T(128)}, f32[3,256,1536]{2,1,0:T(8,128)}, s32[72]{0:T(128)S(1)}, bf16[3,256,3072]{2,1,0:T(8,128)(2,1)}, bf16[24,3,128,128]{3,2,1,0:T(8,128)(2,1)}, /*index=5*/s32[]{:T(128)}, f32[]{:T(128)}) while((s32[]{:T(128)}, f32[3,256,1536]{2,1,0:T(8,128)}, s32[72]{0:T(128)S(1)}, bf16[3,256,3072]{2,1,0:T(8,128)(2,1)}, ...), condition=%wide.region_6.7_spmd, body=%wide.region_4.6_spmd.sunk | while | flops 606339264 | bytes 58983860 | solution.py:28
  532.6 15.1 %scatter_fusion.1 = f32[256,12,128]{2,0,1:T(8,128)S(1)} fusion(f32[256,12,128]{2,0,1:T(8,128)S(1)} %broadcast.195, s32[72]{0:T(128)S(1)} %fusion.58, f32[72,256,128]{2,1,0:T(8,128)} %bitcast.189), kind=kCustom, calls=%fused_computation.5.clone.1 | custom fusion | flops 2359296 | bytes 28311840 | tf_op jit(solution)/shard_map/while/body/eval_jaxpr/scatter-add | solution.py:43
  552.1 6.7 fusion.59
  559.0 15.1 %scatter_fusion.1 = f32[256,12,128]{2,0,1:T(8,128)S(1)} fusion(f32[256,12,128]{2,0,1:T(8,128)S(1)} %broadcast.195, s32[72]{0:T(128)S(1)} %fusion.58, f32[72,256,128]{2,1,0:T(8,128)} %bitcast.189), kind=kCustom, calls=%fused_computation.5.clone.1 | custom fusion | flops 2359296 | bytes 28311840 | tf_op jit(solution)/shard_map/while/body/eval_jaxpr/scatter-add | solution.py:43
  585.3 15.0 %scatter_fusion.1 = f32[256,12,128]{2,0,1:T(8,128)S(1)} fusion(f32[256,12,128]{2,0,1:T(8,128)S(1)} %broadcast.195, s32[72]{0:T(128)S(1)} %fusion.58, f32[72,256,128]{2,1,0:T(8,128)} %bitcast.189), kind=kCustom, calls=%fused_computation.5.clone.1 | custom fusion | flops 2359296 | bytes 28311840 | tf_op jit(solution)/shard_map/while/body/eval_jaxpr/scatter-add | solution.py:43
  602.6 62.3 %while.71 = (s32[]{:T(128)}, f32[24,3,128,128]{2,3,1,0:T(8,128)}, bf16[3,256,12,128]{3,1,2,0:T(8,128)(2,1)}, s32[24,3]{1,0:T(8,128)}, bf16[3,256,24,128]{3,2,1,0...) while((s32[]{:T(128)}, f32[24,3,128,128]{2,3,1,0:T(8,128)}, ...), condition=%wide.wide.region_17.20_spmd.clone, body=%wide.wide.region_16.19_spmd.clone.sunk | while | flops 608700032 | bytes 39327380 | solution.py:78
  636.0 7.7 %bitcast_add_fusion.7 = f32[24,3,128,128]{2,3,1,0:T(8,128)} fusion(f32[24,3,128,128]{2,3,1,0:T(8,128)} %get-tuple-element.734, pred[]{:T(512)S(6)} %compare.9, bf16[256,24,3,128]{3,0,2,1:T(8,128)(2,1)} %bitcast.192, bf16[1,256,24,128]{3,2,1,0:T(8,128)(2,1)S(1)} %constant_dynamic-slice_fusion.21), kind=kOutput, calls=%fused_computation.36.clone.clone.1 | convolution fusion | flops 606339072 | bytes 15728641 | tf_op jit(solution)/shard_map/while/body/eval_jaxpr/tik,tiso->isko/dot_general | solution.py:74
  657.2 7.6 %bitcast_add_fusion.7 = f32[24,3,128,128]{2,3,1,0:T(8,128)} fusion(f32[24,3,128,128]{2,3,1,0:T(8,128)} %get-tuple-element.734, pred[]{:T(512)S(6)} %compare.9, bf16[256,24,3,128]{3,0,2,1:T(8,128)(2,1)} %bitcast.192, bf16[1,256,24,128]{3,2,1,0:T(8,128)(2,1)S(1)} %constant_dynamic-slice_fusion.21), kind=kOutput, calls=%fused_computation.36.clone.clone.1 | convolution fusion | flops 606339072 | bytes 15728641 | tf_op jit(solution)/shard_map/while/body/eval_jaxpr/tik,tiso->isko/dot_general | solution.py:74
  675.6 59.9 %while.70 = (s32[]{:T(128)}, f32[12,6,128,128]{2,3,1,0:T(8,128)}, bf16[3,256,24,128]{3,2,1,0:T(8,128)(2,1)}, s32[12,6]{1,0:T(8,128)}, bf16[3,256,12,128]{3,1,2,0...) while((s32[]{:T(128)}, f32[12,6,128,128]{2,3,1,0:T(8,128)}, ...), condition=%wide.wide.region_15.18_spmd.clone, body=%wide.wide.region_14.17_spmd.clone.sunk | while | flops 608700032 | bytes 40114320 | solution.py:78
  707.3 7.8 %bitcast_add_fusion.6 = f32[12,6,128,128]{2,3,1,0:T(8,128)} fusion(f32[12,6,128,128]{2,3,1,0:T(8,128)} %get-tuple-element.710, pred[]{:T(512)S(6)} %compare.8, bf16[256,12,6,128]{3,0,2,1:T(8,128)(2,1)} %bitcast.195, bf16[3,256,12,128]{3,1,2,0:T(8,128)(2,1)} %get-tuple-element.721, s32[]{:T(128)} %get-tuple-element.709), kind=kOutput, calls=%fused_computation.26.clone.clone.1 | convolution fusion | flops 606339072 | bytes 14942721 | tf_op jit(solution)/shard_map/while/body/eval_jaxpr/tik,tiso->isko/dot_general | solution.py:74
  727.8 7.8 %bitcast_add_fusion.6 = f32[12,6,128,128]{2,3,1,0:T(8,128)} fusion(f32[12,6,128,128]{2,3,1,0:T(8,128)} %get-tuple-element.710, pred[]{:T(512)S(6)} %compare.8, bf16[256,12,6,128]{3,0,2,1:T(8,128)(2,1)} %bitcast.195, bf16[3,256,12,128]{3,1,2,0:T(8,128)(2,1)} %get-tuple-element.721, s32[]{:T(128)} %get-tuple-element.709), kind=kOutput, calls=%fused_computation.26.clone.clone.1 | convolution fusion | flops 606339072 | bytes 14942721 | tf_op jit(solution)/shard_map/while/body/eval_jaxpr/tik,tiso->isko/dot_general | solution.py:74
  (215 shorter events, 322.5 us)
Async XLA Ops:
  7.2 39.3 %all-gather.9.cloned.1.call-start = ((), (), s32[]{:S(2)}) async-start(), calls=%async_computation.8 | async-start | bytes 2506752 | tf_op jit(solution)/shard_map/all_gather | solution.py:83
  7.9 102.8 %all-gather.5.cloned.1.call-start = ((), (), s32[]{:S(2)}) async-start(), calls=%async_computation.4 | async-start | bytes 2506752 | tf_op jit(solution)/shard_map/all_gather | solution.py:83
  8.6 226.5 %reduce-scatter.9.cloned.1.call-start = ((), (), s32[]{:S(2)}) async-start(), calls=%async_computation.9 | async-start | bytes 10616832 | tf_op jit(solution)/shard_map/reduce_scatter | solution.py:91
  9.5 41.8 %copy-start.1 = (s32[24,3]{1,0:T(8,128)}, s32[24,3]{1,0:T(8,128)S(1)}, u32[]{:S(2)}) copy-start(s32[24,3]{1,0:T(8,128)S(1)} %broadcast_subtract_fusion) | copy-start | bytes 868
  109.8 0.7 copy-start.5
  109.8 251.9 %reduce-scatter.5.cloned.1.call-start = ((), (), s32[]{:S(2)}) async-start(), calls=%async_computation.5 | async-start | bytes 10616832 | tf_op jit(solution)/shard_map/reduce_scatter | solution.py:91
  110.6 255.4 %copy-start.3 = (s32[12,6]{1,0:T(8,128)}, s32[12,6]{1,0:T(8,128)S(1)}, u32[]{:S(2)}) copy-start(s32[12,6]{1,0:T(8,128)S(1)} %broadcast_subtract_fusion.1) | copy-start | bytes 868
  207.4 231.8 %all-gather.11.cloned.1.call-start = ((), (), s32[]{:S(2)}) async-start(), calls=%async_computation.10 | async-start | bytes 5308416 | tf_op jit(solution)/shard_map/all_gather | solution.py:87
  365.2 149.8 %all-gather.7.cloned.1.call-start = ((), (), s32[]{:S(2)}) async-start(), calls=%async_computation.6 | async-start | bytes 5308416 | tf_op jit(solution)/shard_map/all_gather | solution.py:87
  365.8 374.7 %reduce-scatter.11.cloned.1.call-start = ((), (), s32[]{:S(2)}) async-start(), calls=%async_computation.11 | async-start | bytes 5013504 | tf_op jit(solution)/shard_map/reduce_scatter | solution.py:97
  491.8 0.7 copy-start.2
  491.8 0.8 copy-start.4
  491.8 250.2 %reduce-scatter.7.cloned.1.call-start = ((), (), s32[]{:S(2)}) async-start(), calls=%async_computation.7 | async-start | bytes 5013504 | tf_op jit(solution)/shard_map/reduce_scatter | solution.py:97
  493.3 9.5 %copy-start = (bf16[3,256,1536]{2,1,0:T(8,128)(2,1)S(1)}, bf16[3,256,1536]{2,1,0:T(8,128)(2,1)}, u32[]{:S(2)}) copy-start(bf16[3,256,1536]{2,1,0:T(8,128)(2,1)} %get-tuple-element.769) | copy-start | bytes 7077892
  669.7 5.9 copy-start.6
Sparse Core Ops, SparseCore 0:
  9.7 36.6 all-gather.8
  48.1 34.3 all-gather.4
  109.9 125.2 reduce-scatter.8
  238.9 122.7 reduce-scatter.4
  365.3 73.7 all-gather.10
  441.3 73.6 all-gather.6
  517.4 66.2 reduce-scatter.10
  602.7 66.4 reduce-scatter.6
where the time goes:
time: 754 us; the launch traced here: 751 us
  waiting for transfers between devices  271 us (36%)
  local copies, waits for them, and re-layouts  210 us (28%)
  other arithmetic  145 us (19%)
  matrix products  109 us (14%)
  between operations  14.2 us (2%)
    reduce_scatter x2, waiting for transfers between devices, col_partial(): lax.psum_scatter(term_fn(jnp.int32(0), height * lax.axis_size('col')), 'c...  154 us
    scatter-add x6, other arithmetic, spread_one_block(): placed = jnp.zeros((height, out_blocks, values.shape[3]), jnp.float32).at...  90.7 us
    all_gather x2, waiting for transfers between devices, col_panel(): return lax.all_gather(local_rows, 'col', axis=0, tiled=True)  78.2 us
    dot_general x6, matrix products, accumulate(): jnp.einsum('tik,tiso->isko', left_part, picked, preferred_element_type=jn...  43.6 us
    dot_general x6, matrix products, spread_one_block(): jnp.einsum('tik,isko->tiso', shaped, values, preferred_element_type=jnp.f...  40.6 us
    all_gather x2, waiting for transfers between devices, row_panel(): return lax.all_gather(local_rows, 'row', axis=0, tiled=True)  36.9 us
    dynamic_update_slice x24, local copies, waits for them, and re-layouts, blocked(): result = lax.map(apply_block, stacked)  36.1 us
    gather x6, local copies, waits for them, and re-layouts, accumulate(): picked = jnp.take(right_part, local_index.reshape(-1), axis=1)  33.4 us
  transfers between devices with their start and end apart: 8, of which 5 were waited for; matrix products, arithmetic and copies ran while one was open for 61% of the time, Pallas kernels for 0%

commit v1 on v0

v1 whole, which is shorter than its diff:
```python
import jax
import jax.numpy as jnp
from jax import lax
from jax.experimental import pallas as pl
from jax.experimental.pallas import tpu as pltpu
from jax.sharding import PartitionSpec as P

MESH = pl.DeviceIdType.MESH
gelu_scale = 0.7978845608028654
gelu_cubic = 0.044715

BLK = 128
CW = 256
NQ = 12
NU = 2 * NQ
NS = 8
NP = 4
SH = 96
RY = 64
OWN = 48
DW = 1536
S2, S3, S4, A2, A3, A4 = 2, 3, 4, 5, 6, 7
TICKS = NU + A4


def gelu_pair(pre_act):
    inner_arg = gelu_scale * (pre_act + gelu_cubic * pre_act * pre_act * pre_act)
    tanh_value = jnp.tanh(inner_arg)
    activated = 0.5 * pre_act * (1.0 + tanh_value)
    derivative = 0.5 * (1.0 + tanh_value) + 0.5 * pre_act * (
        1.0 - tanh_value * tanh_value
    ) * gelu_scale * (1.0 + 3.0 * gelu_cubic * pre_act * pre_act)
    return (activated, derivative)


def f32(v):
    return v.astype(jnp.float32)


def bf16(v):
    return v.astype(jnp.bfloat16)


def dot(a, b, ca, cb):
    return lax.dot_general(a, b, (((ca,), (cb,)), ((), ())), preferred_element_type=jnp.float32)


def kernel(
    inv1, inv2, pick1, pick2, x_in, c_in, v1_hbm, v2_hbm,
    out_ref, ig_ref, fg_ref, sg_ref,
    panel, cblk, xt, v1, v2, wd1, wd2, part, sy_y, szo_y, sz_y, szo_z, sz_z, sy_z,
    ry_y, rzo_y, rz_y, rzo_z, rz_z, ry_z,
    gath, deriv, acc, fgd, rd, rq, ro, rx, ryl, tf,
    v_sem, rs_s, rs_r, ag_s, ag_r, rg_s, rg_r, rr_s, rr_r,
):
    row, col = lax.axis_index("row"), lax.axis_index("col")
    x, yl, core = row // 4, (row // 2) % 2, row % 2
    z, y = col // 2, col % 2
    zp, zm, zo = (z + 1) % 4, (z + 3) % 4, (z + 2) % 4
    xp, xm, xo = (x + 1) % 4, (x + 3) % 4, (x + 2) % 4
    yo, ylo, co = 1 - y, 1 - yl, 1 - core

    def at_row(ax, ayl, ac):
        return (ax * 2 + ayl) * 2 + ac

    dev_z = ((row, zp * 2 + y), (row, zm * 2 + y))
    dev_y = (row, z * 2 + yo)
    dev_x = ((at_row(xp, yl, core), col), (at_row(xm, yl, core), col))
    dev_yl = (at_row(x, ylo, core), col)
    dev_c = (at_row(x, yl, co), col)

    barrier = pltpu.get_barrier_semaphore()
    for dev in (*dev_z, dev_y, *dev_x, dev_yl, dev_c):
        pl.semaphore_signal(barrier, inc=1, device_id=dev, device_id_type=MESH)

    def copy(src, dst, send, recv, dev):
        return pltpu.make_async_remote_copy(
            src_ref=src, dst_ref=dst, send_sem=send, recv_sem=recv, device_id=dev, device_id_type=MESH
        )

    load1 = pltpu.make_async_copy(v1_hbm, v1.at[pl.ds(0, 72)], v_sem.at[0])
    load2 = pltpu.make_async_copy(v2_hbm, v2.at[pl.ds(0, 72)], v_sem.at[1])
    load1.start()
    load2.start()
    v1[72] = jnp.zeros((BLK, BLK), jnp.bfloat16)
    v2[72] = jnp.zeros((BLK, BLK), jnp.bfloat16)
    panel[0, row] = x_in[...]
    panel[1, row] = c_in[...]
    acc[...] = jnp.zeros(acc.shape, jnp.float32)
    pl.semaphore_wait(barrier, 7)

    halves = (pl.ds(0, DW // 2), pl.ds(DW // 2, DW // 2))

    def rg(p, k, src, dev):
        return copy(src, src, rg_s.at[p, k], rg_r.at[p, k], dev)

    def rg_piece(p, ax, ayl, ac=None):
        return panel.at[p, at_row(ax, ayl, core if ac is None else ac)]

    near, far = (xm, xp), (xp, xm)

    order = [(x, yl), (x, ylo), (xm, yl), (xp, yl), (xm, ylo), (xp, ylo), (xo, yl), (xo, ylo)]

    def to_core(p, i):
        return rg(p, 9 + i, rg_piece(p, *order[i]), dev_c)

    def gather_step(p, step):
        if step == 0:
            own = rg_piece(p, x, yl)
            rg(p, 0, own, dev_yl).start()
            for d in range(2):
                rg(p, 1 + d, own, dev_x[d]).start()
            to_core(p, 0).start()
        if step == 1:
            rg(p, 0, rg_piece(p, x, ylo), dev_yl).wait_recv()
            other = rg_piece(p, x, ylo)
            for d in range(2):
                rg(p, 3 + d, other, dev_x[d]).start()
            to_core(p, 1).start()
        if step in (2, 3):
            side = (yl, ylo)[step - 2]
            for d in range(2):
                piece = rg_piece(p, near[d], side)
                rg(p, 1 + 2 * (step - 2) + d, piece, dev_x[d]).wait_recv()
                half = piece.at[:, halves[d]]
                rg(p, 5 + 2 * (step - 2) + d, half, dev_x[d]).start()
                to_core(p, 2 + 2 * (step - 2) + d).start()
        if step == 4:
            for s, side in enumerate((yl, ylo)):
                for d in range(2):
                    half = rg_piece(p, xo, side).at[:, halves[d]]
                    rg(p, 5 + 2 * s + d, half, dev_x[d]).wait_recv()
                to_core(p, 6 + s).start()
        if step == 5:
            own = rg_piece(p, x, yl)
            rg(p, 0, own, dev_yl).wait_send()
            for s, side in enumerate((yl, ylo)):
                for d in range(2):
                    rg(p, 1 + 2 * s + d, rg_piece(p, x, side), dev_x[d]).wait_send()
                    half = rg_piece(p, near[d], side).at[:, halves[d]]
                    rg(p, 5 + 2 * s + d, half, dev_x[d]).wait_send()
            for i in range(8):
                to_core(p, i).wait_send()
                rg(p, 9 + i, rg_piece(p, *order[i], co), dev_c).wait_recv()

    for step in range(6):
        gather_step(0, step)
    load1.wait()
    load2.wait()
    xt[...] = panel[0].reshape(16 * OWN, DW).T

    def dense1(q):
        for i in range(12):
            for h in range(2):
                wd1[pl.ds(i * BLK, BLK), pl.ds(h * BLK, BLK)] = v1[inv1[i, q * 2 + h]]
        return wd1[...]

    def dense2(q):
        for h in range(2):
            for i in range(12):
                wd2[pl.ds(h * BLK, BLK), pl.ds(i * BLK, BLK)] = v2[inv2[q * 2 + h, i]]
        return wd2[...]

    ya, za = pl.ds(0, RY), pl.ds(RY, SH - RY)
    hc = (pl.ds(0, CW // 2), pl.ds(CW // 2, CW // 2))
    tgt = (zp, zm)

    def rs(s, k, src, dst, dev):
        return copy(src, dst, rs_s.at[s, k], rs_r.at[s, k], dev)

    def rs_y_y(u):
        return rs(u % NS, 0, sy_y.at[u % 2], ry_y.at[u % NS], dev_y)

    def rs_zo_y(u, d):
        return rs(u % NS, 1 + d, szo_y.at[u % 2, d], rzo_y.at[u % NS, d], dev_z[d])

    def rs_z_y(u, d):
        return rs(u % NS, 3 + d, sz_y.at[u % 2, d], rz_y.at[u % NS, d], dev_z[d])

    def rs_zo_z(u, d):
        return rs(u % NS, 5 + d, szo_z.at[u % 2, d], rzo_z.at[u % NS, d], dev_z[d])

    def rs_z_z(u, d):
        return rs(u % NS, 7 + d, sz_z.at[u % 2, d], rz_z.at[u % NS, d], dev_z[d])

    def rs_y_z(u):
        return rs(u % NS, 9, sy_z.at[u % 2], ry_z.at[u % NS], dev_y)

    def ag(s, k, ref, dev):
        return copy(ref, ref, ag_s.at[s, k], ag_r.at[s, k], dev)

    src_z = (zm, zp)

    def ag_y_y(s, side):
        return ag(s, 0, gath.at[s, z, side, ya], dev_y)

    def ag_z_y(s, d, at):
        return ag(s, 1 + d, gath.at[s, at, :, ya], dev_z[d])

    def ag_zo_y(s, d, at):
        return ag(s, 3 + d, gath.at[s, at, :, ya, hc[d]], dev_z[d])

    def ag_z_z(s, d, at):
        return ag(s, 5 + d, gath.at[s, at, y, za], dev_z[d])

    def ag_zo_z(s, d, at):
        return ag(s, 7 + d, gath.at[s, at, y, za, hc[d]], dev_z[d])

    def ag_y_z(s, side):
        return ag(s, 9, gath.at[s, :, side, za], dev_y)

    def product(u):
        sp, s2 = u % NP, u % 2

        @pl.when(u < NQ)
        def _():
            r = dot(panel[0].reshape(16 * OWN, DW), dense1(u), 1, 0)
            part[sp] = r.reshape(4, 2, SH, CW)

        @pl.when(u >= NQ)
        def _():
            r = dot(panel[1].reshape(16 * OWN, DW), dense2(u - NQ), 1, 1)
            part[sp] = r.reshape(4, 2, SH, CW)

        sy_y[s2] = bf16(part[sp, :, yo, ya])
        rs_y_y(u).start()
        for d in range(2):
            szo_z[s2, d] = bf16(part[sp, zo, :, za, hc[d]])
            rs_zo_z(u, d).start()

    def stage2(u):
        s, sp, s2 = u % NS, u % NP, u % 2
        rs_y_y(u).wait()
        for d in range(2):
            szo_y[s2, d] = bf16(part[sp, zo, y, ya, hc[d]] + f32(ry_y[s, zo, :, hc[d]]))
            rs_zo_y(u, d).start()
        for d in range(2):
            rs_zo_z(u, d).wait()
            sz_z[s2, d, :, :, hc[d]] = bf16(part[sp, tgt[d], :, za, hc[d]] + f32(rzo_z[s, d]))
            sz_z[s2, d, :, :, hc[1 - d]] = bf16(part[sp, tgt[d], :, za, hc[1 - d]])
            rs_z_z(u, d).start()

    def stage3(u):
        s, sp, s2 = u % NS, u % NP, u % 2
        for d in range(2):
            rs_zo_y(u, d).wait()
            for e in range(2):
                total = part[sp, tgt[d], y, ya, hc[e]] + f32(ry_y[s, tgt[d], :, hc[e]])
                if e == d:
                    total = total + f32(rzo_y[s, d])
                sz_y[s2, d, :, hc[e]] = bf16(total)
            rs_z_y(u, d).start()
        for d in range(2):
            rs_z_z(u, d).wait()
        sy_z[s2] = bf16(part[sp, z, yo, za] + f32(rz_z[s, 0, yo]) + f32(rz_z[s, 1, yo]))
        rs_y_z(u).start()

    def stage4(u):
        s, sp = u % NS, u % NP
        for d in range(2):
            rs_z_y(u, d).wait()
        sum_y = part[sp, z, y, ya] + f32(ry_y[s, z]) + f32(rz_y[s, 0]) + f32(rz_y[s, 1])
        rs_y_z(u).wait()
        sum_z = part[sp, z, y, za] + f32(rz_z[s, 0, y]) + f32(rz_z[s, 1, y]) + f32(ry_z[s])

        @pl.when(u < NQ)
        def _():
            for rows, total in ((ya, sum_y), (za, sum_z)):
                activated, derivative = gelu_pair(total)
                gath[s, z, y, rows] = bf16(activated)
                deriv[u, rows] = derivative

        @pl.when(u >= NQ)
        def _():
            for rows, total in ((ya, sum_y), (za, sum_z)):
                gath[s, z, y, rows] = bf16(total * deriv[u - NQ, rows])

        ag_y_y(s, y).start()
        for d in range(2):
            ag_z_z(s, d, z).start()

    def gather2(u):
        s = u % NS
        ag_y_y(s, yo).wait_recv()
        for d in range(2):
            ag_z_y(s, d, z).start()
        for d in range(2):
            ag_z_z(s, d, src_z[d]).wait_recv()
            ag_zo_z(s, d, src_z[d]).start()

    def gather3(u):
        s = u % NS
        for d in range(2):
            ag_z_y(s, d, src_z[d]).wait_recv()
            ag_zo_y(s, d, src_z[d]).start()
        for d in range(2):
            ag_zo_z(s, d, zo).wait_recv()
        ag_y_z(s, y).start()

    def gather4(u):
        s = u % NS
        for d in range(2):
            ag_zo_y(s, d, zo).wait_recv()
        ag_y_z(s, yo).wait_recv()
        ag_y_y(s, y).wait_send()
        ag_y_z(s, y).wait_send()
        for d in range(2):
            ag_z_y(s, d, z).wait_send()
            ag_zo_y(s, d, src_z[d]).wait_send()
            ag_z_z(s, d, z).wait_send()
            ag_zo_z(s, d, src_z[d]).wait_send()

    def use(u):
        s = u % NS

        @pl.when(u < NQ)
        def _():
            hidden = gath[s].reshape(8 * SH, CW)
            r = dot(hidden, dense2(u), 1, 0)
            acc[0] += r.reshape(8, 2, OWN, DW)
            flipped = hidden.T
            for h in range(2):
                j = u * 2 + h
                picked = jnp.concatenate(
                    [
                        cblk[pick2[j, k]]
                        for k in range(3)
                    ],
                    axis=1,
                )
                g = bf16(dot(flipped[h * BLK : (h + 1) * BLK], picked, 1, 0))
                for k in range(3):
                    sg_ref[j, k] = g[:, k * BLK : (k + 1) * BLK]

        @pl.when(u >= NQ)
        def _():
            q = u - NQ
            grad = gath[s].reshape(8 * SH, CW)
            r = dot(grad, dense1(q), 1, 1)
            acc[1] += r.reshape(8, 2, OWN, DW)
            g = bf16(dot(xt[...], grad, 1, 0))
            for h in range(2):
                fgd[q * 2 + h] = g[:, h * BLK : (h + 1) * BLK]

    hd = (pl.ds(0, DW // 2), pl.ds(DW // 2, DW // 2))
    tgt_x = (xp, xm)

    def rr(p, k, src, dst, dev):
        return copy(src, dst, rr_s.at[p, k], rr_r.at[p, k], dev)

    def rr_core(p):
        return rr(p, 0, acc.at[p, :, co], rd.at[p], dev_c)

    def rr_xo(p, d):
        return rr(p, 1 + d, rq.at[xo, :, :, hd[d]], ro.at[p, d], dev_x[d])

    def rr_x(p, d):
        return rr(p, 3 + d, rq.at[tgt_x[d]], rx.at[p, d], dev_x[d])

    def rr_yl(p):
        return rr(p, 5, tf, ryl.at[p], dev_yl)

    def own_sum(p, ax, ayl):
        return acc[p, ax * 2 + ayl, core] + rd[p, ax * 2 + ayl]

    def scatter_step(p, step):
        if step == 0:
            rr_core(p).start()
        if step == 1:
            rr_core(p).wait()
            for at in (xo, xp, xm):
                for b in range(2):
                    rq[at, b] = bf16(own_sum(p, at, b))
                if at is xo:
                    for d in range(2):
                        rr_xo(p, d).start()
        if step == 2:
            for d in range(2):
                rr_xo(p, d).wait()
                for b in range(2):
                    own = acc[p, tgt_x[d] * 2 + b, core, :, hd[d]] + rd[p, tgt_x[d] * 2 + b, :, hd[d]]
                    rq[tgt_x[d], b, :, hd[d]] = bf16(own + f32(ro[p, d, b]))
                rr_x(p, d).start()
        if step == 3:
            for d in range(2):
                rr_x(p, d).wait()
            tf[...] = bf16(own_sum(p, x, ylo) + f32(rx[p, 0, ylo]) + f32(rx[p, 1, ylo]))
            rr_yl(p).start()
        if step == 4:
            rr_yl(p).wait()
            total = own_sum(p, x, yl) + f32(rx[p, 0, yl]) + f32(rx[p, 1, yl]) + f32(ryl[p])
            (out_ref, ig_ref)[p][...] = bf16(total)

    def tick(t, carry):
        def run(offset, fn):
            u = t - offset

            @pl.when(jnp.logical_and(u >= 0, u < NU))
            def _():
                fn(u)

        run(A4, gather4)
        run(A3, gather3)
        run(A2, gather2)
        run(S4, stage4)
        run(S3, stage3)
        run(S2, stage2)
        for step in range(6):
            @pl.when(t == 1 + step)
            def _():
                gather_step(1, step)
        @pl.when(t == 7)
        def _():
            for c in range(12):
                cblk[c] = panel[1, :, :, c * BLK : (c + 1) * BLK].reshape(16 * OWN, BLK)

        for step in range(5):
            @pl.when(t == NQ + A4 + step)
            def _():
                scatter_step(0, step)
        run(0, product)
        run(A4, use)
        return carry

    lax.fori_loop(0, TICKS, tick, 0)
    scatter_step(1, 0)
    for i in range(12):
        for k in range(6):
            fg_ref[i, k] = fgd[pick1[i, k], pl.ds(i * BLK, BLK), :]
    for step in range(1, 5):
        scatter_step(1, step)


def shards(inputs, first_values, first_blocks, second_values, second_blocks, cotangent):
    pick1 = first_blocks - lax.axis_index("row") * 24
    pick2 = second_blocks - lax.axis_index("col") * 12

    def slot_table(pick, width):
        rows, slots = pick.shape
        number = jnp.arange(rows * slots, dtype=jnp.int32).reshape(rows, slots) - rows * slots
        hit = pick[:, :, None] == jnp.arange(width, dtype=jnp.int32)
        return rows * slots + jnp.sum(jnp.where(hit, number[:, :, None], 0), axis=1)

    inv1 = slot_table(pick1, 24)
    inv2 = slot_table(pick2, 12)
    bf, fl = jnp.bfloat16, jnp.float32
    smem = pl.BlockSpec(memory_space=pltpu.SMEM)
    vmem = pl.BlockSpec(memory_space=pltpu.VMEM)
    dma = pltpu.SemaphoreType.DMA
    v1 = first_values.reshape(72, BLK, BLK)
    v2 = second_values.reshape(72, BLK, BLK)
    return pl.pallas_call(
        kernel,
        out_shape=(
            jax.ShapeDtypeStruct((OWN, DW), bf),
            jax.ShapeDtypeStruct((OWN, DW), bf),
            jax.ShapeDtypeStruct((12, 6, BLK, BLK), bf),
            jax.ShapeDtypeStruct((24, 3, BLK, BLK), bf),
        ),
        in_specs=[smem] * 4 + [vmem] * 2 + [pl.BlockSpec(memory_space=pl.ANY)] * 2,
        out_specs=(vmem,) * 4,
        scratch_shapes=[
            pltpu.VMEM((2, 16, OWN, DW), bf),
            pltpu.VMEM((12, 16 * OWN, BLK), bf),
            pltpu.VMEM((DW, 16 * OWN), bf),
            pltpu.VMEM((73, BLK, BLK), bf),
            pltpu.VMEM((73, BLK, BLK), bf),
            pltpu.VMEM((DW, CW), bf),
            pltpu.VMEM((CW, DW), bf),
            pltpu.VMEM((NP, 4, 2, SH, CW), fl),
            pltpu.VMEM((2, 4, RY, CW), bf),
            pltpu.VMEM((2, 2, RY, CW // 2), bf),
            pltpu.VMEM((2, 2, RY, CW), bf),
            pltpu.VMEM((2, 2, 2, SH - RY, CW // 2), bf),
            pltpu.VMEM((2, 2, 2, SH - RY, CW), bf),
            pltpu.VMEM((2, SH - RY, CW), bf),
            pltpu.VMEM((NS, 4, RY, CW), bf),
            pltpu.VMEM((NS, 2, RY, CW // 2), bf),
            pltpu.VMEM((NS, 2, RY, CW), bf),
            pltpu.VMEM((NS, 2, 2, SH - RY, CW // 2), bf),
            pltpu.VMEM((NS, 2, 2, SH - RY, CW), bf),
            pltpu.VMEM((NS, SH - RY, CW), bf),
            pltpu.VMEM((NS, 4, 2, SH, CW), bf),
            pltpu.VMEM((NQ, SH, CW), fl),
            pltpu.VMEM((2, 8, 2, OWN, DW), fl),
            pltpu.VMEM((24, DW, BLK), bf),
            pltpu.VMEM((2, 8, OWN, DW), fl),
            pltpu.VMEM((4, 2, OWN, DW), bf),
            pltpu.VMEM((2, 2, 2, OWN, DW // 2), bf),
            pltpu.VMEM((2, 2, 2, OWN, DW), bf),
            pltpu.VMEM((2, OWN, DW), bf),
            pltpu.VMEM((OWN, DW), bf),
            dma((2,)),
            dma((NS, 10)), dma((NS, 10)), dma((NS, 10)), dma((NS, 10)),
            dma((2, 17)), dma((2, 17)), dma((2, 6)), dma((2, 6)),
        ],
        compiler_params=pltpu.CompilerParams(
            collective_id=1, has_side_effects=True, vmem_limit_bytes=62 * 2**20
        ),
        name="sparse_ffn",
    )(inv1, inv2, pick1, pick2, inputs, cotangent, v1, v2)


def solution(mesh):
    placed = (
        P("row", "col"),
        P("col", "row", None, None),
        P("col", "row"),
        P("row", "col", None, None),
        P("row", "col"),
        P("row", "col"),
    )
    return jax.shard_map(
        shards,
        mesh=mesh,
        in_specs=placed,
        out_specs=(
            P("row", "col"),
            P("row", "col"),
            P("col", "row", None, None),
            P("row", "col", None, None),
        ),
        check_vma=False,
    )
```

time: 754 us -> 218 us (0.29)
  waiting for transfers between devices: 271 us -> 0 us
  Pallas kernels: 0 us -> 206 us
  local copies, waits for them, and re-layouts: 210 us -> 9.79 us
  other arithmetic: 145 us -> 1.35 us
  matrix products: 109 us -> 0 us
  between operations: 14.2 us -> 0.66 us
    pallas_call x0 -> x1, Pallas kernels: none -> 206 us  [shards(): pl.pallas_call(kernel, out_shape=(jax.ShapeDtypeStruct((OWN, DW), bf), ja...]
    reduce_scatter x4 -> x0, waiting for transfers between devices: 154 us -> none  [the longest x2 154 us: col_partial(): lax.psum_scatter(term_fn(jnp.int32(0), height * lax.axis_size('col')), 'c...]
    all_gather x4 -> x0, waiting for transfers between devices: 115 us -> none  [the longest x2 78.2 us: col_panel(): return lax.all_gather(local_rows, 'col', axis=0, tiled=True)]
    dot_general x18 -> x0, matrix products: 109 us -> none  [the longest x6 43.6 us: accumulate(): jnp.einsum('tik,tiso->isko', left_part, picked, preferred_element_type=jn...]
    scatter-add x6 -> x0, other arithmetic: 90.7 us -> none  [spread_one_block(): placed = jnp.zeros((height, out_blocks, values.shape[3]), jnp.float32).at...]
    gather x12 -> x0, local copies, waits for them, and re-layouts: 66.7 us -> none  [the longest x6 33.4 us: accumulate(): picked = jnp.take(right_part, local_index.reshape(-1), axis=1)]
    select_n x30 -> x0, other arithmetic: 47.3 us -> none  [the longest x12 30.3 us: accumulate(): picked = jnp.take(right_part, local_index.reshape(-1), axis=1)]
    dynamic_update_slice x24 -> x0, local copies, waits for them, and re-layouts: 36.1 us -> none  [blocked(): result = lax.map(apply_block, stacked)]
  transfers between devices with their start and end apart: 8 -> 0, of which waited for: 5 -> 0; matrix products, arithmetic and copies ran while one was open for 61% -> 0% of each run, Pallas kernels for 0% -> 0%
where the time goes in v1:
time: 218 us
  Pallas kernels  206 us (94%)
  local copies, waits for them, and re-layouts  9.79 us (4%)
    pallas_call x1, Pallas kernels, shards(): pl.pallas_call(kernel, out_shape=(jax.ShapeDtypeStruct((OWN, DW), bf), ja...  206 us
    unnamed x12, local copies, waits for them, and re-layouts  9.62 us

profile of v1, /device:TPU:0, one launch (start us, length us, event | category | flops | bytes accessed | tf_op | source)
XLA Modules:
  0.0 217.6 jit_solution(943500238047669381)
XLA Ops:
  0.6 0.8 copy.16
  1.4 0.0 copy-start.2
  1.4 0.1 select_reduce_fusion
  1.5 0.6 broadcast_add_fusion.1.inv1
  2.1 0.8 copy.17
  2.9 0.0 copy-start.1
  2.9 0.1 copy.19
  3.0 0.1 copy.20
  3.1 0.6 broadcast_add_fusion.inv2
  3.7 0.0 copy-done.2
  3.7 0.0 copy-done.1
  3.7 205.8 %sparse_ffn.1 = (bf16[48,1536]{1,0:T(8,128)(2,1)}, bf16[48,1536]{1,0:T(8,128)(2,1)}, bf16[12,6,128,128]{3,2,1,0:T(8,128)(2,1)}, bf16[24,3,128,128]{3,2,1,0:T(8,128)(2,1)}) custom-call(s32[12,24]{1,0:T(8,128)} %broadcast_add_fusion.1.inv1, s32[24,12]{1,0:T(8,128)} %broadcast_add_fusion.inv2, s32[12,6]{1,0:T(8,128)} %copy-done.2, s32[24,3]{1,0:T(8,128)} %copy-done.1, ...), custom_call_target="tpu_custom_call" | custom-call | tf_op jit(solution)/shard_map/sparse_ffn/pallas_call | solution.py:452
  209.5 1.6 copy.26
  211.1 1.6 copy.27
  212.7 0.0 copy-start
  212.7 3.5 %copy.28 = bf16[12,6,128,128]{3,2,1,0:T(8,128)(2,1)} copy(bf16[12,6,128,128]{3,2,1,0:T(8,128)(2,1)} %get-tuple-element.12) | data formatting | bytes 4718592
  216.2 0.0 copy-done
  216.2 1.4 copy.29
  (4 shorter events, 0.0 us)
Async XLA Ops:
  1.4 2.3 %copy-start.2 = (s32[12,6]{1,0:T(8,128)}, s32[12,6]{1,0:T(8,128)S(1)}, u32[]{:S(2)}) copy-start(s32[12,6]{1,0:T(8,128)S(1)} %get-tuple-element.5.pick1) | copy-start | bytes 868
  2.9 0.8 copy-start.1
  212.7 3.5 %copy-start = (bf16[24,3,128,128]{3,2,1,0:T(8,128)(2,1)S(1)}, bf16[24,3,128,128]{3,2,1,0:T(8,128)(2,1)}, u32[]{:S(2)}) copy-start(bf16[24,3,128,128]{3,2,1,0:T(8,128)(2,1)} %get-tuple-element.13) | copy-start | bytes 7077892

commit v2 on v0

v2 whole, which is shorter than its diff:
```python
import jax
import jax.numpy as jnp
from jax import lax
from jax.experimental import pallas as pl
from jax.experimental.pallas import tpu as pltpu
from jax.sharding import PartitionSpec as P

MESH = pl.DeviceIdType.MESH
gelu_scale = 0.7978845608028654
gelu_cubic = 0.044715

BLK = 128
NG = 3
NC = 4
CB = 6
CW = CB * BLK
NN = NG * NC
NU = 2 * NN
NS = 12
NA = 13
NT = 3
NP = 9
GR = 16
SR = 2 * GR
OWN = NG * GR
DW = 1536
S2, S3, S4 = 3, 6, 9
A2, A3, A4 = 3, 6, 9
AG1, AG2 = NN + 1, 3 * NN
TICKS = AG2 + NN + A4
SG = AG1 + 2 * NN + A4 - 1


def gelu_pair(pre_act):
    inner_arg = gelu_scale * (pre_act + gelu_cubic * pre_act * pre_act * pre_act)
    tanh_value = jnp.tanh(inner_arg)
    activated = 0.5 * pre_act * (1.0 + tanh_value)
    derivative = 0.5 * (1.0 + tanh_value) + 0.5 * pre_act * (
        1.0 - tanh_value * tanh_value
    ) * gelu_scale * (1.0 + 3.0 * gelu_cubic * pre_act * pre_act)
    return (activated, derivative)


def f32(v):
    return v.astype(jnp.float32)


def bf16(v):
    return v.astype(jnp.bfloat16)


def dot(a, b, ca, cb):
    return lax.dot_general(a, b, (((ca,), (cb,)), ((), ())), preferred_element_type=jnp.float32)


def kernel(
    inv1, inv2, pick1, pick2, x_in, c_in, v1_hbm, v2_hbm,
    out_ref, ig_ref, fg_ref, sg_ref,
    panel, cblk, xt, v1, v2, wd1, wd2, part, sy_y, szo_y, sz_y, szo_z, sz_z, sy_z,
    ry_y, rzo_y, rz_y, rzo_z, rz_z, ry_z,
    gath, deriv, acc, rd, rq, rx, ryl, tf, sgb, fgb,
    v_sem, rs_s, rs_r, ag_s, ag_r, rg_s, rg_r, rr_s, rr_r,
):
    row, col = lax.axis_index("row"), lax.axis_index("col")
    x, yl, core = row // 4, (row // 2) % 2, row % 2
    z, y = col // 2, col % 2
    zp, zm, zo = (z + 1) % 4, (z + 3) % 4, (z + 2) % 4
    xp, xm, xo = (x + 1) % 4, (x + 3) % 4, (x + 2) % 4
    yo, ylo, co = 1 - y, 1 - yl, 1 - core

    def at_row(ax, ayl, ac):
        return (ax * 2 + ayl) * 2 + ac

    dev_z = ((row, zp * 2 + y), (row, zm * 2 + y))
    dev_y = (row, z * 2 + yo)
    dev_row = [(at_row(ax, yl, core), col) for ax in (xp, xm, xo)]
    dev_row += [(at_row(ax, ylo, core), col) for ax in (x, xp, xm, xo)]
    dev_row += [(at_row(x, yl, co), col)]

    barrier = pltpu.get_barrier_semaphore()
    for dev in (*dev_z, dev_y, *dev_row):
        pl.semaphore_signal(barrier, inc=1, device_id=dev, device_id_type=MESH)

    def copy(src, dst, send, recv, dev):
        return pltpu.make_async_remote_copy(
            src_ref=src, dst_ref=dst, send_sem=send, recv_sem=recv, device_id=dev, device_id_type=MESH
        )

    load1 = pltpu.make_async_copy(v1_hbm, v1.at[pl.ds(0, 72)], v_sem.at[0])
    load2 = pltpu.make_async_copy(v2_hbm, v2.at[pl.ds(0, 72)], v_sem.at[1])
    load1.start()
    load2.start()
    for g in range(NG):
        panel[0, g, row] = x_in[pl.ds(g * GR, GR)]
        panel[1, g, row] = c_in[pl.ds(g * GR, GR)]
    pl.semaphore_wait(barrier, 11)


    order = [(x, yl), (x, ylo), (xp, yl), (xm, yl), (xo, yl), (xp, ylo), (xm, ylo), (xo, ylo)]
    all_x = (xp, xm, xo)
    from_x = (xm, xp, xo)

    def gather_step(p, g, step, direct=False):
        def rg(k, src, ax, ayl, ac=core):
            return copy(src, src, rg_s.at[p, g, k], rg_r.at[p, g, k], (at_row(ax, ayl, ac), col))

        def piece(ax, ayl, ac=core):
            return panel.at[p, g, at_row(ax, ayl, ac)]

        def over_yl(side):
            return rg(0, piece(x, side), x, ylo)

        def own_x(d, at):
            return rg(1 + d, piece(at, yl), all_x[d], yl)

        def other_x(d, at):
            if direct:
                return rg(4 + d, piece(at, ylo if at is not x else yl), all_x[d], ylo)
            return rg(4 + d, piece(at, ylo), all_x[d], yl)

        def to_core(i, ac=core):
            return rg(7 + i, piece(*order[i], ac), x, yl, co)

        if step == 0:
            over_yl(yl).start()
            for d in range(3):
                own_x(d, x).start()
            if direct:
                for d in range(3):
                    other_x(d, x).start()
            to_core(0).start()
        if step == 1:
            over_yl(ylo).wait_recv()
            if not direct:
                for d in range(3):
                    other_x(d, x).start()
            to_core(1).start()
        if step == 2:
            for d in range(3):
                own_x(d, from_x[d]).wait_recv()
                to_core(2 + (1, 0, 2)[d]).start()
        if step == 3:
            for d in range(3):
                other_x(d, from_x[d]).wait_recv()
                to_core(5 + (1, 0, 2)[d]).start()
        if step == 4:
            over_yl(yl).wait_send()
            for d in range(3):
                own_x(d, x).wait_send()
                other_x(d, x).wait_send()
            for i in range(8):
                to_core(i).wait_send()
                to_core(i, co).wait_recv()

    for step in range(5):
        gather_step(0, 0, step, direct=True)
        if step == 0:
            v1[72] = jnp.zeros((BLK, BLK), jnp.bfloat16)
            v2[72] = jnp.zeros((BLK, BLK), jnp.bfloat16)
            acc[...] = jnp.zeros(acc.shape, jnp.float32)
        if step == 1:
            gather_step(0, 1, 0)
        if step == 3:
            gather_step(0, 1, 1)
            gather_step(0, 2, 0)
    load1.wait()
    load2.wait()

    def dense1(c):
        for i in range(12):
            for h in range(CB):
                wd1[pl.ds(i * BLK, BLK), pl.ds(h * BLK, BLK)] = v1[inv1[i, c * CB + h]]
        return wd1[...]

    def dense2(c):
        for h in range(CB):
            for i in range(12):
                wd2[pl.ds(h * BLK, BLK), pl.ds(i * BLK, BLK)] = v2[inv2[c * CB + h, i]]
        return wd2[...]

    ya, za = pl.ds(0, GR), pl.ds(GR, GR)
    hc = (pl.ds(0, CW // 2), pl.ds(CW // 2, CW // 2))
    tgt, src_z = (zp, zm), (zm, zp)

    def rs(u, k, src, dst, dev):
        return copy(src, dst, rs_s.at[u % NS, k], rs_r.at[u % NS, k], dev)

    def rs_y_y(u):
        return rs(u, 0, sy_y.at[u % NT], ry_y.at[u % NS], dev_y)

    def rs_zo_y(u, d):
        return rs(u, 1 + d, szo_y.at[u % NT, d], rzo_y.at[u % NS, d], dev_z[d])

    def rs_z_y(u, d):
        return rs(u, 3 + d, sz_y.at[u % NT, d], rz_y.at[u % NS, d], dev_z[d])

    def rs_zo_z(u, d):
        return rs(u, 5 + d, szo_z.at[u % NT, d], rzo_z.at[u % NS, d], dev_z[d])

    def rs_z_z(u, d):
        return rs(u, 7 + d, sz_z.at[u % NT, d], rz_z.at[u % NS, d], dev_z[d])

    def rs_y_z(u):
        return rs(u, 9, sy_z.at[u % NT], ry_z.at[u % NS], dev_y)

    def product(u):
        sp, s2 = u % NP, u % NT
        g, c = (u // NC) % NG, u % NC

        @pl.when(u < NN)
        def _():
            r = dot(panel[0, g].reshape(16 * GR, DW), dense1(c), 1, 0)
            part[sp] = r.reshape(4, 2, SR, CW)

        @pl.when(u >= NN)
        def _():
            r = dot(panel[1, g].reshape(16 * GR, DW), dense2(c), 1, 1)
            part[sp] = r.reshape(4, 2, SR, CW)

        sy_y[s2] = bf16(part[sp, :, yo, ya])
        rs_y_y(u).start()
        for d in range(2):
            szo_z[s2, d] = bf16(part[sp, zo, :, za, hc[d]])
            rs_zo_z(u, d).start()

    def stage2(u):
        s, sp, s2 = u % NS, u % NP, u % NT
        rs_y_y(u).wait()
        for d in range(2):
            szo_y[s2, d] = bf16(part[sp, zo, y, ya, hc[d]] + f32(ry_y[s, zo, :, hc[d]]))
            rs_zo_y(u, d).start()
        for d in range(2):
            rs_zo_z(u, d).wait()
            sz_z[s2, d, :, :, hc[d]] = bf16(part[sp, tgt[d], :, za, hc[d]] + f32(rzo_z[s, d]))
            sz_z[s2, d, :, :, hc[1 - d]] = bf16(part[sp, tgt[d], :, za, hc[1 - d]])
            rs_z_z(u, d).start()

    def stage3(u):
        s, sp, s2 = u % NS, u % NP, u % NT
        for d in range(2):
            rs_zo_y(u, d).wait()
            for e in range(2):
                total = part[sp, tgt[d], y, ya, hc[e]] + f32(ry_y[s, tgt[d], :, hc[e]])
                if e == d:
                    total = total + f32(rzo_y[s, d])
                sz_y[s2, d, :, hc[e]] = bf16(total)
            rs_z_y(u, d).start()
        for d in range(2):
            rs_z_z(u, d).wait()
        sy_z[s2] = bf16(part[sp, z, yo, za] + f32(rz_z[s, 0, yo]) + f32(rz_z[s, 1, yo]))
        rs_y_z(u).start()

    def stage4(u):
        s, sp = u % NS, u % NP
        g, c = (u // NC) % NG, u % NC
        for d in range(2):
            rs_z_y(u, d).wait()
        sum_y = part[sp, z, y, ya] + f32(ry_y[s, z]) + f32(rz_y[s, 0]) + f32(rz_y[s, 1])
        rs_y_z(u).wait()
        sum_z = part[sp, z, y, za] + f32(rz_z[s, 0, y]) + f32(rz_z[s, 1, y]) + f32(ry_z[s])

        def keep(p, rows, value):
            for b in range(CB):
                gath[p, c * CB + b, g, z, y, rows] = bf16(value[:, b * BLK : (b + 1) * BLK])

        @pl.when(u < NN)
        def _():
            for rows, total in ((ya, sum_y), (za, sum_z)):
                activated, derivative = gelu_pair(total)
                keep(0, rows, activated)
                deriv[u, rows] = derivative

        @pl.when(u >= NN)
        def _():
            for rows, total in ((ya, sum_y), (za, sum_z)):
                keep(1, rows, total * deriv[u - NN, rows])

    def ag_of(u):
        p, g, c = u // NN, (u // NC) % NG, u % NC
        yb = gath.at[p, pl.ds(c * CB, 4), g]
        zb = gath.at[p, pl.ds(c * CB + 4, 2), g]
        yh = (gath.at[p, pl.ds(c * CB, 2), g], gath.at[p, pl.ds(c * CB + 2, 2), g])
        zh = (gath.at[p, pl.ds(c * CB + 4, 1), g], gath.at[p, pl.ds(c * CB + 5, 1), g])

        def ag(k, ref, dev):
            return copy(ref, ref, ag_s.at[u % NA, k], ag_r.at[u % NA, k], dev)

        return (
            lambda side: ag(0, yb.at[:, z, side], dev_y),
            lambda d, at: ag(1 + d, yb.at[:, at], dev_z[d]),
            lambda d, at: ag(3 + d, yh[d].at[:, at], dev_z[d]),
            lambda d, at: ag(5 + d, zb.at[:, at, y], dev_z[d]),
            lambda d, at: ag(7 + d, zh[d].at[:, at, y], dev_z[d]),
            lambda side: ag(9, zb.at[:, :, side], dev_y),
        )

    def gather1(u):
        y_y, z_y, zo_y, z_z, zo_z, y_z = ag_of(u)
        y_y(y).start()
        for d in range(2):
            z_z(d, z).start()

    def gather2(u):
        y_y, z_y, zo_y, z_z, zo_z, y_z = ag_of(u)
        y_y(yo).wait_recv()
        for d in range(2):
            z_y(d, z).start()
        for d in range(2):
            z_z(d, src_z[d]).wait_recv()
            zo_z(d, src_z[d]).start()

    def gather3(u):
        y_y, z_y, zo_y, z_z, zo_z, y_z = ag_of(u)
        for d in range(2):
            z_y(d, src_z[d]).wait_recv()
            zo_y(d, src_z[d]).start()
        for d in range(2):
            zo_z(d, zo).wait_recv()
        y_z(y).start()

    def gather4(u):
        y_y, z_y, zo_y, z_z, zo_z, y_z = ag_of(u)
        for d in range(2):
            zo_y(d, zo).wait_recv()
        y_z(yo).wait_recv()
        y_y(y).wait_send()
        y_z(y).wait_send()
        for d in range(2):
            z_y(d, z).wait_send()
            zo_y(d, src_z[d]).wait_send()
            z_z(d, z).wait_send()
            zo_z(d, src_z[d]).wait_send()

    def use(u):
        p, g, c = u // NN, (u // NC) % NG, u % NC
        rows = jnp.concatenate([gath[p, c * CB + b, g].reshape(16 * GR, BLK) for b in range(CB)], axis=1)

        @pl.when(p == 0)
        def _():
            acc[0, g] += dot(rows, dense2(c), 1, 0).reshape(8, 2, GR, DW)

        @pl.when(p == 1)
        def _():
            acc[1, g] += dot(rows, dense1(c), 1, 1).reshape(8, 2, GR, DW)

    def second_out(j):
        return pltpu.make_async_copy(sgb.at[j % 2], sg_ref.at[j], v_sem.at[2 + j % 2])

    def second(j):
        flipped = gath[0, j].reshape(16 * OWN, BLK).T
        picked = jnp.concatenate([cblk[pick2[j, k]] for k in range(3)], axis=1)
        g = bf16(dot(flipped, picked, 1, 0))

        @pl.when(j >= 2)
        def _():
            second_out(j - 2).wait()

        for k in range(3):
            sgb[j % 2, k] = g[:, k * BLK : (k + 1) * BLK]
        second_out(j).start()

    def first_out(i):
        return pltpu.make_async_copy(fgb.at[i % 2], fg_ref.at[i], v_sem.at[4 + i % 2])

    def first(i):
        picked = jnp.concatenate([gath[1, pick1[i, k]].reshape(16 * OWN, BLK) for k in range(6)], axis=1)
        g = bf16(dot(xt[pl.ds(i * BLK, BLK), :], picked, 1, 0))
        if i >= 2:
            first_out(i - 2).wait()
        for k in range(6):
            fgb[i % 2, k] = g[:, k * BLK : (k + 1) * BLK]
        first_out(i).start()

    def scatter_step(p, g, step, direct=False):
        e = p * NG + g

        def rr(k, src, dst, ax, ayl, ac=core):
            return copy(src, dst, rr_s.at[e, k], rr_r.at[e, k], (at_row(ax, ayl, ac), col))

        def over_core():
            return rr(0, acc.at[p, g, :, co], rd.at[g], x, yl, co)

        def over_x(d, b=None):
            if b is None:
                return rr(1 + d, rq.at[g, all_x[d]], rx.at[g, d], all_x[d], yl)
            return rr(1 + 2 * d + b, rq.at[g, all_x[d], (yl, ylo)[b]], rx.at[g, d, b], all_x[d], (yl, ylo)[b])

        def over_yl():
            return rr(7, tf.at[g], ryl.at[g], x, ylo)

        def own_sum(ax, ayl):
            return acc[p, g, ax * 2 + ayl, core] + rd[g, ax * 2 + ayl]

        if step == 0:
            over_core().start()
        if step == 1:
            over_core().wait()
            if direct:
                tf[g] = bf16(own_sum(x, ylo))
                over_yl().start()
            for d in (2, 0, 1):
                for b in range(2):
                    rq[g, all_x[d], b] = bf16(own_sum(all_x[d], b))
                if direct:
                    for b in range(2):
                        over_x(d, b).start()
                else:
                    over_x(d).start()
        if step == 2 and not direct:
            for d in range(3):
                over_x(d).wait()
            tf[g] = bf16(own_sum(x, ylo) + f32(rx[g, 0, ylo]) + f32(rx[g, 1, ylo]) + f32(rx[g, 2, ylo]))
            over_yl().start()
        if step == 3:
            total = own_sum(x, yl)
            for d in range(3):
                if direct:
                    for b in range(2):
                        over_x(d, b).wait()
                        total = total + f32(rx[g, d, b])
                else:
                    total = total + f32(rx[g, d, yl])
            over_yl().wait()
            total = bf16(total + f32(ryl[g]))
            rows = pl.ds(pl.multiple_of(g * GR, GR), GR)

            @pl.when(p == 0)
            def _():
                out_ref[rows, :] = total

            @pl.when(p == 1)
            def _():
                ig_ref[rows, :] = total

    def rs_unit(t):
        late = t - NN
        u = jnp.where(t < NN, t, NN + late // 2)
        return u, (t >= 0) & (t < 3 * NN) & ((t < NN) | (late % 2 == 0))

    def ag_unit(t):
        early = t - AG1
        u = jnp.where(t < AG2, early // 2, NN + t - AG2)
        return u, ((t >= AG1) & (t < AG2) & (early % 2 == 0)) | ((t >= AG2) & (t < AG2 + NN))

    def at_ticks(steps):
        def find(t):
            n, ok = jnp.int32(0), jnp.bool_(False)
            for e, at in steps:
                n = n + jnp.where(t == at, e, 0)
                ok = ok | (t == at)
            return n, ok

        return find

    gathers = [
        (1, (None, None, 0, 2, 4)),
        (2, (None, 2, 4, 6, 8)),
        (3, (1, 4, 7, 9, 12)),
        (4, (7, 10, 13, 16, 19)),
        (5, (13, 16, 19, 22, 25)),
    ]
    scatters = [(g, AG1 + 2 * (NC * g + NC - 1) + A4 + 1) for g in range(NG)]
    scatters += [(NG + g, AG2 + NC * g + NC - 1 + A4 + 1) for g in range(NG - 1)]
    scatters = [(e, tuple(start + 2 * k for k in range(4))) for e, start in scatters]

    def tick(t, carry):
        def run(offset, unit_of, fn):
            u, ok = unit_of(t - offset)

            @pl.when(ok)
            def _():
                fn(u)

        run(A4, ag_unit, gather4)
        run(A3, ag_unit, gather3)
        run(A2, ag_unit, gather2)
        run(S4, rs_unit, stage4)
        run(0, ag_unit, gather1)
        run(S3, rs_unit, stage3)
        run(S2, rs_unit, stage2)
        for step in range(4, -1, -1):
            run(0, at_ticks([(e, ticks[step]) for e, ticks in gathers if ticks[step] is not None]),
                lambda e, step=step: gather_step(e // NG, e % NG, step))
        for step in range(3, -1, -1):
            run(0, at_ticks([(e, ticks[step]) for e, ticks in scatters if ticks[step] < TICKS]),
                lambda e, step=step: scatter_step(e // NG, e % NG, step))
        run(0, rs_unit, product)
        run(A4, ag_unit, use)

        @pl.when(t == 28)
        def _():
            for c in range(12):
                cblk[c] = panel[1, :, :, :, c * BLK : (c + 1) * BLK].reshape(16 * OWN, BLK)

        @pl.when(t == 30)
        def _():
            xt[...] = panel[0].reshape(16 * OWN, DW).T

        @pl.when((t >= SG) & (t < SG + 12))
        def _():
            second(2 * (t - SG))
            second(2 * (t - SG) + 1)

        return carry

    lax.fori_loop(0, TICKS, tick, 0)
    scatter_step(1, NG - 1, 0, direct=True)
    for e, ticks in scatters:
        for step in range(4):
            if ticks[step] >= TICKS:
                scatter_step(e // NG, e % NG, step)
    first(0)
    scatter_step(1, NG - 1, 1, direct=True)
    for i in range(1, 12):
        first(i)
    scatter_step(1, NG - 1, 3, direct=True)
    for i in range(2):
        second_out(22 + i).wait()
        first_out(10 + i).wait()


def shards(inputs, first_values, first_blocks, second_values, second_blocks, cotangent):
    pick1 = first_blocks - lax.axis_index("row") * 24
    pick2 = second_blocks - lax.axis_index("col") * 12

    def slot_table(pick, width):
        rows, slots = pick.shape
        number = jnp.arange(rows * slots, dtype=jnp.int32).reshape(rows, slots) - rows * slots
        hit = pick[:, :, None] == jnp.arange(width, dtype=jnp.int32)
        return rows * slots + jnp.sum(jnp.where(hit, number[:, :, None], 0), axis=1)

    inv1 = slot_table(pick1, 24)
    inv2 = slot_table(pick2, 12)
    bf, fl = jnp.bfloat16, jnp.float32
    smem = pl.BlockSpec(memory_space=pltpu.SMEM)
    vmem = pl.BlockSpec(memory_space=pltpu.VMEM)
    dma = pltpu.SemaphoreType.DMA
    v1 = first_values.reshape(72, BLK, BLK)
    v2 = second_values.reshape(72, BLK, BLK)
    return pl.pallas_call(
        kernel,
        out_shape=(
            jax.ShapeDtypeStruct((OWN, DW), bf),
            jax.ShapeDtypeStruct((OWN, DW), bf),
            jax.ShapeDtypeStruct((12, 6, BLK, BLK), bf),
            jax.ShapeDtypeStruct((24, 3, BLK, BLK), bf),
        ),
        in_specs=[smem] * 4 + [vmem] * 2 + [pl.BlockSpec(memory_space=pl.ANY)] * 2,
        out_specs=(vmem,) * 2 + (pl.BlockSpec(memory_space=pl.ANY),) * 2,
        scratch_shapes=[
            pltpu.VMEM((2, NG, 16, GR, DW), bf),
            pltpu.VMEM((12, 16 * OWN, BLK), bf),
            pltpu.VMEM((DW, 16 * OWN), bf),
            pltpu.VMEM((73, BLK, BLK), bf),
            pltpu.VMEM((73, BLK, BLK), bf),
            pltpu.VMEM((DW, CW), bf),
            pltpu.VMEM((CW, DW), bf),
            pltpu.VMEM((NP, 4, 2, SR, CW), fl),
            pltpu.VMEM((NT, 4, GR, CW), bf),
            pltpu.VMEM((NT, 2, GR, CW // 2), bf),
            pltpu.VMEM((NT, 2, GR, CW), bf),
            pltpu.VMEM((NT, 2, 2, GR, CW // 2), bf),
            pltpu.VMEM((NT, 2, 2, GR, CW), bf),
            pltpu.VMEM((NT, GR, CW), bf),
            pltpu.VMEM((NS, 4, GR, CW), bf),
            pltpu.VMEM((NS, 2, GR, CW // 2), bf),
            pltpu.VMEM((NS, 2, GR, CW), bf),
            pltpu.VMEM((NS, 2, 2, GR, CW // 2), bf),
            pltpu.VMEM((NS, 2, 2, GR, CW), bf),
            pltpu.VMEM((NS, GR, CW), bf),
            pltpu.VMEM((2, NC * CB, NG, 4, 2, SR, BLK), bf),
            pltpu.VMEM((NN, SR, CW), fl),
            pltpu.VMEM((2, NG, 8, 2, GR, DW), fl),
            pltpu.VMEM((NG, 8, GR, DW), fl),
            pltpu.VMEM((NG, 4, 2, GR, DW), bf),
            pltpu.VMEM((NG, 3, 2, GR, DW), bf),
            pltpu.VMEM((NG, GR, DW), bf),
            pltpu.VMEM((NG, GR, DW), bf),
            pltpu.VMEM((2, 3, BLK, BLK), bf),
            pltpu.VMEM((2, 6, BLK, BLK), bf),
            dma((6,)),
            dma((NS, 10)), dma((NS, 10)), dma((NA, 10)), dma((NA, 10)),
            dma((2, NG, 15)), dma((2, NG, 15)), dma((2 * NG, 8)), dma((2 * NG, 8)),
        ],
        compiler_params=pltpu.CompilerParams(
            collective_id=1, has_side_effects=True, vmem_limit_bytes=62 * 2**20
        ),
        name="sparse_ffn",
    )(inv1, inv2, pick1, pick2, inputs, cotangent, v1, v2)


def solution(mesh):
    placed = (
        P("row", "col"),
        P("col", "row", None, None),
        P("col", "row"),
        P("row", "col", None, None),
        P("row", "col"),
        P("row", "col"),
    )
    return jax.shard_map(
        shards,
        mesh=mesh,
        in_specs=placed,
        out_specs=(
            P("row", "col"),
            P("row", "col"),
            P("col", "row", None, None),
            P("row", "col", None, None),
        ),
        check_vma=False,
    )
```

time: 754 us -> 187 us (0.25)
  waiting for transfers between devices: 271 us -> 0 us
  local copies, waits for them, and re-layouts: 210 us -> 9.79 us
  Pallas kernels: 0 us -> 175 us
  other arithmetic: 145 us -> 1.35 us
  matrix products: 109 us -> 0 us
  between operations: 14.2 us -> 0.66 us
    pallas_call x0 -> x1, Pallas kernels: none -> 175 us  [shards(): pl.pallas_call(kernel, out_shape=(jax.ShapeDtypeStruct((OWN, DW), bf), ja...]
    reduce_scatter x4 -> x0, waiting for transfers between devices: 154 us -> none  [the longest x2 154 us: col_partial(): lax.psum_scatter(term_fn(jnp.int32(0), height * lax.axis_size('col')), 'c...]
    all_gather x4 -> x0, waiting for transfers between devices: 115 us -> none  [the longest x2 78.2 us: col_panel(): return lax.all_gather(local_rows, 'col', axis=0, tiled=True)]
    dot_general x18 -> x0, matrix products: 109 us -> none  [the longest x6 43.6 us: accumulate(): jnp.einsum('tik,tiso->isko', left_part, picked, preferred_element_type=jn...]
    scatter-add x6 -> x0, other arithmetic: 90.7 us -> none  [spread_one_block(): placed = jnp.zeros((height, out_blocks, values.shape[3]), jnp.float32).at...]
    gather x12 -> x0, local copies, waits for them, and re-layouts: 66.7 us -> none  [the longest x6 33.4 us: accumulate(): picked = jnp.take(right_part, local_index.reshape(-1), axis=1)]
    select_n x30 -> x0, other arithmetic: 47.3 us -> none  [the longest x12 30.3 us: accumulate(): picked = jnp.take(right_part, local_index.reshape(-1), axis=1)]
    dynamic_update_slice x24 -> x0, local copies, waits for them, and re-layouts: 36.1 us -> none  [blocked(): result = lax.map(apply_block, stacked)]
  transfers between devices with their start and end apart: 8 -> 0, of which waited for: 5 -> 0; matrix products, arithmetic and copies ran while one was open for 61% -> 0% of each run, Pallas kernels for 0% -> 0%
where the time goes in v2:
time: 187 us
  Pallas kernels  175 us (94%)
  local copies, waits for them, and re-layouts  9.79 us (5%)
    pallas_call x1, Pallas kernels, shards(): pl.pallas_call(kernel, out_shape=(jax.ShapeDtypeStruct((OWN, DW), bf), ja...  175 us
    unnamed x12, local copies, waits for them, and re-layouts  9.62 us

profile of v2, /device:TPU:0, one launch (start us, length us, event | category | flops | bytes accessed | tf_op | source)
XLA Modules:
  0.0 186.9 jit_solution(17961426924302086404)
XLA Ops:
  0.6 0.8 copy.16
  1.4 0.0 copy-start.2
  1.4 0.1 select_reduce_fusion
  1.5 0.6 broadcast_add_fusion.1.inv1
  2.1 0.8 copy.17
  2.9 0.0 copy-start.1
  2.9 0.1 copy.19
  3.0 0.1 copy.20
  3.1 0.6 broadcast_add_fusion.inv2
  3.7 0.0 copy-done.2
  3.7 0.0 copy-done.1
  3.7 175.1 %sparse_ffn.1 = (bf16[48,1536]{1,0:T(8,128)(2,1)}, bf16[48,1536]{1,0:T(8,128)(2,1)}, bf16[12,6,128,128]{3,2,1,0:T(8,128)(2,1)}, bf16[24,3,128,128]{3,2,1,0:T(8,128)(2,1)}) custom-call(s32[12,24]{1,0:T(8,128)} %broadcast_add_fusion.1.inv1, s32[24,12]{1,0:T(8,128)} %broadcast_add_fusion.inv2, s32[12,6]{1,0:T(8,128)} %copy-done.2, s32[24,3]{1,0:T(8,128)} %copy-done.1, ...), custom_call_target="tpu_custom_call" | custom-call | tf_op jit(solution)/shard_map/sparse_ffn/pallas_call | solution.py:540
  178.8 1.6 copy.26
  180.4 1.6 copy.27
  182.0 0.0 copy-start
  182.0 3.5 %copy.28 = bf16[12,6,128,128]{3,2,1,0:T(8,128)(2,1)} copy(bf16[12,6,128,128]{3,2,1,0:T(8,128)(2,1)} %get-tuple-element.12) | data formatting | bytes 4718592
  185.5 0.0 copy-done
  185.5 1.4 copy.29
  (4 shorter events, 0.0 us)
Async XLA Ops:
  1.4 2.3 %copy-start.2 = (s32[12,6]{1,0:T(8,128)}, s32[12,6]{1,0:T(8,128)S(1)}, u32[]{:S(2)}) copy-start(s32[12,6]{1,0:T(8,128)S(1)} %get-tuple-element.5.pick1) | copy-start | bytes 868
  2.9 0.8 copy-start.1
  182.0 3.5 %copy-start = (bf16[24,3,128,128]{3,2,1,0:T(8,128)(2,1)S(1)}, bf16[24,3,128,128]{3,2,1,0:T(8,128)(2,1)}, u32[]{:S(2)}) copy-start(bf16[24,3,128,128]{3,2,1,0:T(8,128)(2,1)} %get-tuple-element.13) | copy-start | bytes 7077892

commit v3 on v2

--- a/solution.py
+++ b/solution.py
@@ -14,10 +14,13 @@
 NC = 4
 CB = 6
 CW = CB * BLK
+YB = 2
+AB = 4
+YW, ZW = YB * BLK, (CB - YB) * BLK
 NN = NG * NC
 NU = 2 * NN
 NS = 12
-NA = 13
+NR = 7
 NT = 3
 NP = 9
 GR = 16
@@ -54,11 +57,11 @@
 
 
 def kernel(
-    inv1, inv2, pick1, pick2, x_in, c_in, v1_hbm, v2_hbm,
+    blocks1, blocks2, x_in, c_in, v1_hbm, v2_hbm,
     out_ref, ig_ref, fg_ref, sg_ref,
     panel, cblk, xt, v1, v2, wd1, wd2, part, sy_y, szo_y, sz_y, szo_z, sz_z, sy_z,
     ry_y, rzo_y, rz_y, rzo_z, rz_z, ry_z,
-    gath, deriv, acc, rd, rq, rx, ryl, tf, sgb, fgb,
+    gath, deriv, acc, rd, rq, rx, ryl, tf, sgb, fgb, inv1, inv2,
     v_sem, rs_s, rs_r, ag_s, ag_r, rg_s, rg_r, rr_s, rr_r,
 ):
     row, col = lax.axis_index("row"), lax.axis_index("col")
@@ -91,8 +94,8 @@
     load1.start()
     load2.start()
     for g in range(NG):
-        panel[0, g, row] = x_in[pl.ds(g * GR, GR)]
-        panel[1, g, row] = c_in[pl.ds(g * GR, GR)]
+        panel[0, g, row // 2, core] = x_in[pl.ds(g * GR, GR)]
+        panel[1, g, row // 2, core] = c_in[pl.ds(g * GR, GR)]
     pl.semaphore_wait(barrier, 11)
 
 
@@ -101,11 +104,11 @@
     from_x = (xm, xp, xo)
 
     def gather_step(p, g, step, direct=False):
-        def rg(k, src, ax, ayl, ac=core):
-            return copy(src, src, rg_s.at[p, g, k], rg_r.at[p, g, k], (at_row(ax, ayl, ac), col))
-
-        def piece(ax, ayl, ac=core):
-            return panel.at[p, g, at_row(ax, ayl, ac)]
+        def rg(k, src, ax, ayl):
+            return copy(src, src, rg_s.at[p, g, 0], rg_r.at[p, g, k], (at_row(ax, ayl, core), col))
+
+        def piece(ax, ayl):
+            return panel.at[p, g, ax * 2 + ayl, core]
 
         def over_yl(side):
             return rg(0, piece(x, side), x, ylo)
@@ -118,8 +121,11 @@
                 return rg(4 + d, piece(at, ylo if at is not x else yl), all_x[d], ylo)
             return rg(4 + d, piece(at, ylo), all_x[d], yl)
 
-        def to_core(i, ac=core):
-            return rg(7 + i, piece(*order[i], ac), x, yl, co)
+        def core_copy(src):
+            return copy(src, src, rg_s.at[p, g, 1], rg_r.at[p, g, 7], (at_row(x, yl, co), col))
+
+        def to_core(i):
+            return core_copy(piece(*order[i]))
 
         if step == 0:
             over_yl(yl).start()
@@ -144,13 +150,21 @@
                 other_x(d, from_x[d]).wait_recv()
                 to_core(5 + (1, 0, 2)[d]).start()
         if step == 4:
-            over_yl(yl).wait_send()
-            for d in range(3):
-                own_x(d, x).wait_send()
-                other_x(d, x).wait_send()
-            for i in range(8):
-                to_core(i).wait_send()
-                to_core(i, co).wait_recv()
+            rg(0, panel.at[p, g, pl.ds(0, 7), core], x, ylo).wait_send()
+            core_copy(panel.at[p, g, :, core]).wait_send()
+            core_copy(panel.at[p, g, :, co]).wait_recv()
+
+    def slot_table(table, blocks, base, rows, width, slots):
+        def fill(i, carry):
+            names = [blocks[k, i] - base for k in range(slots)]
+            for h in range(width):
+                found = jnp.int32(rows * slots)
+                for k in range(slots):
+                    found = jnp.where(names[k] == h, i * slots + k, found)
+                table[i, h] = found
+            return carry
+
+        lax.fori_loop(0, rows, fill, 0)
 
     for step in range(5):
         gather_step(0, 0, step, direct=True)
@@ -158,6 +172,8 @@
             v1[72] = jnp.zeros((BLK, BLK), jnp.bfloat16)
             v2[72] = jnp.zeros((BLK, BLK), jnp.bfloat16)
             acc[...] = jnp.zeros(acc.shape, jnp.float32)
+            slot_table(inv1, blocks1, row * 24, 12, 24, 6)
+            slot_table(inv2, blocks2, col * 12, 24, 12, 3)
         if step == 1:
             gather_step(0, 1, 0)
         if step == 3:
@@ -178,12 +194,13 @@
                 wd2[pl.ds(h * BLK, BLK), pl.ds(i * BLK, BLK)] = v2[inv2[c * CB + h, i]]
         return wd2[...]
 
-    ya, za = pl.ds(0, GR), pl.ds(GR, GR)
-    hc = (pl.ds(0, CW // 2), pl.ds(CW // 2, CW // 2))
+    yw, zw = pl.ds(0, YW), pl.ds(YW, ZW)
+    yh = (pl.ds(0, YW // 2), pl.ds(YW // 2, YW // 2))
+    zh = (pl.ds(YW, ZW // 2), pl.ds(YW + ZW // 2, ZW // 2))
     tgt, src_z = (zp, zm), (zm, zp)
 
     def rs(u, k, src, dst, dev):
-        return copy(src, dst, rs_s.at[u % NS, k], rs_r.at[u % NS, k], dev)
+        return copy(src, dst, rs_s.at[u % NT, k], rs_r.at[u % NR, k], dev)
 
     def rs_y_y(u):
         return rs(u, 0, sy_y.at[u % NT], ry_y.at[u % NS], dev_y)
@@ -217,22 +234,25 @@
             r = dot(panel[1, g].reshape(16 * GR, DW), dense2(c), 1, 1)
             part[sp] = r.reshape(4, 2, SR, CW)
 
-        sy_y[s2] = bf16(part[sp, :, yo, ya])
+        sy_y[s2] = bf16(part[sp, :, yo, :, yw])
         rs_y_y(u).start()
         for d in range(2):
-            szo_z[s2, d] = bf16(part[sp, zo, :, za, hc[d]])
+            szo_z[s2, d] = bf16(part[sp, zo, :, :, zh[d]])
             rs_zo_z(u, d).start()
 
     def stage2(u):
         s, sp, s2 = u % NS, u % NP, u % NT
         rs_y_y(u).wait()
         for d in range(2):
-            szo_y[s2, d] = bf16(part[sp, zo, y, ya, hc[d]] + f32(ry_y[s, zo, :, hc[d]]))
+            szo_y[s2, d] = bf16(part[sp, zo, y, :, yh[d]] + f32(ry_y[s, zo, :, yh[d]]))
             rs_zo_y(u, d).start()
         for d in range(2):
             rs_zo_z(u, d).wait()
-            sz_z[s2, d, :, :, hc[d]] = bf16(part[sp, tgt[d], :, za, hc[d]] + f32(rzo_z[s, d]))
-            sz_z[s2, d, :, :, hc[1 - d]] = bf16(part[sp, tgt[d], :, za, hc[1 - d]])
+            for e in range(2):
+                total = part[sp, tgt[d], :, :, zh[e]]
+                if e == d:
+                    total = total + f32(rzo_z[s, d])
+                sz_z[s2, d, :, :, pl.ds(e * (ZW // 2), ZW // 2)] = bf16(total)
             rs_z_z(u, d).start()
 
     def stage3(u):
@@ -240,14 +260,14 @@
         for d in range(2):
             rs_zo_y(u, d).wait()
             for e in range(2):
-                total = part[sp, tgt[d], y, ya, hc[e]] + f32(ry_y[s, tgt[d], :, hc[e]])
+                total = part[sp, tgt[d], y, :, yh[e]] + f32(ry_y[s, tgt[d], :, yh[e]])
                 if e == d:
                     total = total + f32(rzo_y[s, d])
-                sz_y[s2, d, :, hc[e]] = bf16(total)
+                sz_y[s2, d, :, yh[e]] = bf16(total)
             rs_z_y(u, d).start()
         for d in range(2):
             rs_z_z(u, d).wait()
-        sy_z[s2] = bf16(part[sp, z, yo, za] + f32(rz_z[s, 0, yo]) + f32(rz_z[s, 1, yo]))
+        sy_z[s2] = bf16(part[sp, z, yo, :, zw] + f32(rz_z[s, 0, yo]) + f32(rz_z[s, 1, yo]))
         rs_y_z(u).start()
 
     def stage4(u):
@@ -255,81 +275,104 @@
         g, c = (u // NC) % NG, u % NC
         for d in range(2):
             rs_z_y(u, d).wait()
-        sum_y = part[sp, z, y, ya] + f32(ry_y[s, z]) + f32(rz_y[s, 0]) + f32(rz_y[s, 1])
+        sum_y = part[sp, z, y, :, yw] + f32(ry_y[s, z]) + f32(rz_y[s, 0]) + f32(rz_y[s, 1])
         rs_y_z(u).wait()
-        sum_z = part[sp, z, y, za] + f32(rz_z[s, 0, y]) + f32(rz_z[s, 1, y]) + f32(ry_z[s])
-
-        def keep(p, rows, value):
-            for b in range(CB):
-                gath[p, c * CB + b, g, z, y, rows] = bf16(value[:, b * BLK : (b + 1) * BLK])
+        sum_z = part[sp, z, y, :, zw] + f32(rz_z[s, 0, y]) + f32(rz_z[s, 1, y]) + f32(ry_z[s])
+
+        def keep(p, first_block, value):
+            for b in range(value.shape[1] // BLK):
+                gath[p, c * CB + first_block + b, g, z, y] = bf16(value[:, b * BLK : (b + 1) * BLK])
 
         @pl.when(u < NN)
         def _():
-            for rows, total in ((ya, sum_y), (za, sum_z)):
+            for lo, cols, total in ((0, yw, sum_y), (YB, zw, sum_z)):
                 activated, derivative = gelu_pair(total)
-                keep(0, rows, activated)
-                deriv[u, rows] = derivative
+                keep(0, lo, activated)
+                deriv[u, :, cols] = derivative
 
         @pl.when(u >= NN)
         def _():
-            for rows, total in ((ya, sum_y), (za, sum_z)):
-                keep(1, rows, total * deriv[u - NN, rows])
-
-    def ag_of(u):
-        p, g, c = u // NN, (u // NC) % NG, u % NC
-        yb = gath.at[p, pl.ds(c * CB, 4), g]
-        zb = gath.at[p, pl.ds(c * CB + 4, 2), g]
-        yh = (gath.at[p, pl.ds(c * CB, 2), g], gath.at[p, pl.ds(c * CB + 2, 2), g])
-        zh = (gath.at[p, pl.ds(c * CB + 4, 1), g], gath.at[p, pl.ds(c * CB + 5, 1), g])
+            for lo, cols, total in ((0, yw, sum_y), (YB, zw, sum_z)):
+                keep(1, lo, total * deriv[u - NN, :, cols])
+
+    def ag_of(u, p):
+        g, c = (u // NC) % NG, u % NC
+
+        def part_of(first_block, blocks, first_row, rows):
+            return lambda at, side: gath.at[
+                p, pl.ds(c * CB + first_block, blocks), g, at, side, pl.ds(first_row, rows)
+            ]
+
+        if p == 0:
+            yb, zb = part_of(0, CB, 0, GR), part_of(0, CB, GR, GR)
+            yhalf = [part_of(d * CB // 2, CB // 2, 0, GR) for d in range(2)]
+            zhalf = [part_of(d * CB // 2, CB // 2, GR, GR) for d in range(2)]
+        else:
+            zb_n = CB - AB
+            yb, zb = part_of(0, AB, 0, SR), part_of(AB, zb_n, 0, SR)
+            yhalf = [part_of(d * AB // 2, AB // 2, 0, SR) for d in range(2)]
+            zhalf = [part_of(AB + d * zb_n // 2, zb_n // 2, 0, SR) for d in range(2)]
+        every = slice(None)
 
         def ag(k, ref, dev):
-            return copy(ref, ref, ag_s.at[u % NA, k], ag_r.at[u % NA, k], dev)
+            return copy(ref, ref, ag_s.at[u % NT, k], ag_r.at[u % NR, k], dev)
 
         return (
-            lambda side: ag(0, yb.at[:, z, side], dev_y),
-            lambda d, at: ag(1 + d, yb.at[:, at], dev_z[d]),
-            lambda d, at: ag(3 + d, yh[d].at[:, at], dev_z[d]),
-            lambda d, at: ag(5 + d, zb.at[:, at, y], dev_z[d]),
-            lambda d, at: ag(7 + d, zh[d].at[:, at, y], dev_z[d]),
-            lambda side: ag(9, zb.at[:, :, side], dev_y),
+            lambda side: ag(0, yb(z, side), dev_y),
+            lambda d, at: ag(1 + d, yb(at, every), dev_z[d]),
+            lambda d, at: ag(3 + d, yhalf[d](at, every), dev_z[d]),
+            lambda d, at: ag(5 + d, zb(at, y), dev_z[d]),
+            lambda d, at: ag(7 + d, zhalf[d](at, y), dev_z[d]),
+            lambda side: ag(9, zb(every, side), dev_y),
         )
 
-    def gather1(u):
-        y_y, z_y, zo_y, z_z, zo_z, y_z = ag_of(u)
+    def either(fn):
+        def run(u):
+            for p in range(2):
+                @pl.when(u // NN == p)
+                def _():
+                    fn(*ag_of(u, p))
+
+        return run
+
+    @either
+    def gather1(y_y, z_y, zo_y, z_z, zo_z, y_z):
         y_y(y).start()
         for d in range(2):
             z_z(d, z).start()
 
-    def gather2(u):
-        y_y, z_y, zo_y, z_z, zo_z, y_z = ag_of(u)
+    @either
+    def gather2(y_y, z_y, zo_y, z_z, zo_z, y_z):
         y_y(yo).wait_recv()
         for d in range(2):
             z_y(d, z).start()
         for d in range(2):
             z_z(d, src_z[d]).wait_recv()
             zo_z(d, src_z[d]).start()
-
-    def gather3(u):
-        y_y, z_y, zo_y, z_z, zo_z, y_z = ag_of(u)
+        y_y(y).wait_send()
+        for d in range(2):
+            z_z(d, z).wait_send()
+
+    @either
+    def gather3(y_y, z_y, zo_y, z_z, zo_z, y_z):
         for d in range(2):
             z_y(d, src_z[d]).wait_recv()
             zo_y(d, src_z[d]).start()
         for d in range(2):
             zo_z(d, zo).wait_recv()
         y_z(y).start()
-
-    def gather4(u):
-        y_y, z_y, zo_y, z_z, zo_z, y_z = ag_of(u)
+        for d in range(2):
+            z_y(d, z).wait_send()
+            zo_z(d, src_z[d]).wait_send()
+
+    @either
+    def gather4(y_y, z_y, zo_y, z_z, zo_z, y_z):
         for d in range(2):
             zo_y(d, zo).wait_recv()
         y_z(yo).wait_recv()
-        y_y(y).wait_send()
         y_z(y).wait_send()
         for d in range(2):
-            z_y(d, z).wait_send()
             zo_y(d, src_z[d]).wait_send()
-            z_z(d, z).wait_send()
-            zo_z(d, src_z[d]).wait_send()
 
     def use(u):
         p, g, c = u // NN, (u // NC) % NG, u % NC
@@ -343,12 +386,15 @@
         def _():
             acc[1, g] += dot(rows, dense1(c), 1, 1).reshape(8, 2, GR, DW)
 
+    def local_block(blocks, i, k, base, width):
+        return jnp.clip(blocks[k, i] - base, 0, width - 1)
+
     def second_out(j):
         return pltpu.make_async_copy(sgb.at[j % 2], sg_ref.at[j], v_sem.at[2 + j % 2])
 
     def second(j):
         flipped = gath[0, j].reshape(16 * OWN, BLK).T
-        picked = jnp.concatenate([cblk[pick2[j, k]] for k in range(3)], axis=1)
+        picked = jnp.concatenate([cblk[local_block(blocks2, j, k, col * 12, 12)] for k in range(3)], axis=1)
         g = bf16(dot(flipped, picked, 1, 0))
 
         @pl.when(j >= 2)
@@ -363,7 +409,7 @@
         return pltpu.make_async_copy(fgb.at[i % 2], fg_ref.at[i], v_sem.at[4 + i % 2])
 
     def first(i):
-        picked = jnp.concatenate([gath[1, pick1[i, k]].reshape(16 * OWN, BLK) for k in range(6)], axis=1)
+        picked = jnp.concatenate([gath[1, local_block(blocks1, i, k, row * 24, 24)].reshape(16 * OWN, BLK) for k in range(6)], axis=1)
         g = bf16(dot(xt[pl.ds(i * BLK, BLK), :], picked, 1, 0))
         if i >= 2:
             first_out(i - 2).wait()
@@ -375,7 +421,8 @@
         e = p * NG + g
 
         def rr(k, src, dst, ax, ayl, ac=core):
-            return copy(src, dst, rr_s.at[e, k], rr_r.at[e, k], (at_row(ax, ayl, ac), col))
+            send = rr_s.at[e, 0 if k == 0 else 2 if k == 7 else 1]
+            return copy(src, dst, send, rr_r.at[e, k], (at_row(ax, ayl, ac), col))
 
         def over_core():
             return rr(0, acc.at[p, g, :, co], rd.at[g], x, yl, co)
@@ -387,6 +434,9 @@
 
         def over_yl():
             return rr(7, tf.at[g], ryl.at[g], x, ylo)
+
+        def sent():
+            rr(1, rq.at[g, pl.ds(0, 3)], rx.at[g], xp, yl).wait_send()
 
         def own_sum(ax, ayl):
             return acc[p, g, ax * 2 + ayl, core] + rd[g, ax * 2 + ayl]
@@ -408,7 +458,8 @@
                     over_x(d).start()
         if step == 2 and not direct:
             for d in range(3):
-                over_x(d).wait()
+                over_x(d).wait_recv()
+            sent()
             tf[g] = bf16(own_sum(x, ylo) + f32(rx[g, 0, ylo]) + f32(rx[g, 1, ylo]) + f32(rx[g, 2, ylo]))
             over_yl().start()
         if step == 3:
@@ -416,10 +467,12 @@
             for d in range(3):
                 if direct:
                     for b in range(2):
-                        over_x(d, b).wait()
+                        over_x(d, b).wait_recv()
                         total = total + f32(rx[g, d, b])
                 else:
                     total = total + f32(rx[g, d, yl])
+            if direct:
+                sent()
             over_yl().wait()
             total = bf16(total + f32(ryl[g]))
             rows = pl.ds(pl.multiple_of(g * GR, GR), GR)
@@ -490,7 +543,7 @@
         @pl.when(t == 28)
         def _():
             for c in range(12):
-                cblk[c] = panel[1, :, :, :, c * BLK : (c + 1) * BLK].reshape(16 * OWN, BLK)
+                cblk[c] = panel[1, :, :, :, :, c * BLK : (c + 1) * BLK].reshape(16 * OWN, BLK)
 
         @pl.when(t == 30)
         def _():
@@ -519,25 +572,34 @@
         first_out(10 + i).wait()
 
 
+def hand_over(*refs):
+    ins, outs, bufs, (sem_in, sem_out) = refs[:4], refs[4:8], refs[8:12], refs[12:]
+    loads, stores = [], []
+    for src, dst, buf in zip(ins, outs, bufs):
+        pieces = 6 if len(src.shape) == 4 else 1
+        size = src.shape[0] // pieces
+        for k in range(pieces):
+            rows = pl.ds(k * size, size)
+            n = len(loads)
+            loads.append(pltpu.make_async_copy(src.at[rows], buf.at[rows], sem_in.at[n]))
+            stores.append(pltpu.make_async_copy(buf.at[rows], dst.at[rows], sem_out.at[n]))
+    for load in loads:
+        load.start()
+    for load, store in zip(loads, stores):
+        load.wait()
+        store.start()
+    for store in stores:
+        store.wait()
+
+
 def shards(inputs, first_values, first_blocks, second_values, second_blocks, cotangent):
-    pick1 = first_blocks - lax.axis_index("row") * 24
-    pick2 = second_blocks - lax.axis_index("col") * 12
-
-    def slot_table(pick, width):
-        rows, slots = pick.shape
-        number = jnp.arange(rows * slots, dtype=jnp.int32).reshape(rows, slots) - rows * slots
-        hit = pick[:, :, None] == jnp.arange(width, dtype=jnp.int32)
-        return rows * slots + jnp.sum(jnp.where(hit, number[:, :, None], 0), axis=1)
-
-    inv1 = slot_table(pick1, 24)
-    inv2 = slot_table(pick2, 12)
     bf, fl = jnp.bfloat16, jnp.float32
     smem = pl.BlockSpec(memory_space=pltpu.SMEM)
     vmem = pl.BlockSpec(memory_space=pltpu.VMEM)
     dma = pltpu.SemaphoreType.DMA
     v1 = first_values.reshape(72, BLK, BLK)
     v2 = second_values.reshape(72, BLK, BLK)
-    return pl.pallas_call(
+    results = pl.pallas_call(
         kernel,
         out_shape=(
             jax.ShapeDtypeStruct((OWN, DW), bf),
@@ -545,10 +607,10 @@
             jax.ShapeDtypeStruct((12, 6, BLK, BLK), bf),
             jax.ShapeDtypeStruct((24, 3, BLK, BLK), bf),
         ),
-        in_specs=[smem] * 4 + [vmem] * 2 + [pl.BlockSpec(memory_space=pl.ANY)] * 2,
+        in_specs=[smem] * 2 + [vmem] * 2 + [pl.BlockSpec(memory_space=pl.ANY)] * 2,
         out_specs=(vmem,) * 2 + (pl.BlockSpec(memory_space=pl.ANY),) * 2,
         scratch_shapes=[
-            pltpu.VMEM((2, NG, 16, GR, DW), bf),
+            pltpu.VMEM((2, NG, 8, 2, GR, DW), bf),
             pltpu.VMEM((12, 16 * OWN, BLK), bf),
             pltpu.VMEM((DW, 16 * OWN), bf),
             pltpu.VMEM((73, BLK, BLK), bf),
@@ -556,18 +618,18 @@
             pltpu.VMEM((DW, CW), bf),
             pltpu.VMEM((CW, DW), bf),
             pltpu.VMEM((NP, 4, 2, SR, CW), fl),
-            pltpu.VMEM((NT, 4, GR, CW), bf),
-            pltpu.VMEM((NT, 2, GR, CW // 2), bf),
-            pltpu.VMEM((NT, 2, GR, CW), bf),
-            pltpu.VMEM((NT, 2, 2, GR, CW // 2), bf),
-            pltpu.VMEM((NT, 2, 2, GR, CW), bf),
-            pltpu.VMEM((NT, GR, CW), bf),
-            pltpu.VMEM((NS, 4, GR, CW), bf),
-            pltpu.VMEM((NS, 2, GR, CW // 2), bf),
-            pltpu.VMEM((NS, 2, GR, CW), bf),
-            pltpu.VMEM((NS, 2, 2, GR, CW // 2), bf),
-            pltpu.VMEM((NS, 2, 2, GR, CW), bf),
-            pltpu.VMEM((NS, GR, CW), bf),
+            pltpu.VMEM((NT, 4, SR, YW), bf),
+            pltpu.VMEM((NT, 2, SR, YW // 2), bf),
+            pltpu.VMEM((NT, 2, SR, YW), bf),
+            pltpu.VMEM((NT, 2, 2, SR, ZW // 2), bf),
+            pltpu.VMEM((NT, 2, 2, SR, ZW), bf),
+            pltpu.VMEM((NT, SR, ZW), bf),
+            pltpu.VMEM((NS, 4, SR, YW), bf),
+            pltpu.VMEM((NS, 2, SR, YW // 2), bf),
+            pltpu.VMEM((NS, 2, SR, YW), bf),
+            pltpu.VMEM((NS, 2, 2, SR, ZW // 2), bf),
+            pltpu.VMEM((NS, 2, 2, SR, ZW), bf),
+            pltpu.VMEM((NS, SR, ZW), bf),
             pltpu.VMEM((2, NC * CB, NG, 4, 2, SR, BLK), bf),
             pltpu.VMEM((NN, SR, CW), fl),
             pltpu.VMEM((2, NG, 8, 2, GR, DW), fl),
@@ -578,15 +640,26 @@
             pltpu.VMEM((NG, GR, DW), bf),
             pltpu.VMEM((2, 3, BLK, BLK), bf),
             pltpu.VMEM((2, 6, BLK, BLK), bf),
+            pltpu.SMEM((12, 24), jnp.int32),
+            pltpu.SMEM((24, 12), jnp.int32),
             dma((6,)),
-            dma((NS, 10)), dma((NS, 10)), dma((NA, 10)), dma((NA, 10)),
-            dma((2, NG, 15)), dma((2, NG, 15)), dma((2 * NG, 8)), dma((2 * NG, 8)),
+            dma((NT, 10)), dma((NR, 10)), dma((NT, 10)), dma((NR, 10)),
+            dma((2, NG, 2)), dma((2, NG, 8)), dma((2 * NG, 3)), dma((2 * NG, 8)),
         ],
         compiler_params=pltpu.CompilerParams(
             collective_id=1, has_side_effects=True, vmem_limit_bytes=62 * 2**20
         ),
         name="sparse_ffn",
-    )(inv1, inv2, pick1, pick2, inputs, cotangent, v1, v2)
+    )(first_blocks.T, second_blocks.T, inputs, cotangent, v1, v2)
+    anywhere = pl.BlockSpec(memory_space=pl.ANY)
+    return pl.pallas_call(
+        hand_over,
+        out_shape=tuple(jax.ShapeDtypeStruct(r.shape, r.dtype) for r in results),
+        in_specs=[anywhere] * 4,
+        out_specs=(anywhere,) * 4,
+        scratch_shapes=[pltpu.VMEM(r.shape, r.dtype) for r in results] + [dma((14,)), dma((14,))],
+        name="hand_over",
+    )(*results)
 
 
 def solution(mesh):

time: 187 us -> 174 us (0.930)
  local copies, waits for them, and re-layouts: 9.79 us -> 0 us
  Pallas kernels: 175 us -> 173 us
    unnamed x12 -> x0, local copies, waits for them, and re-layouts: 9.62 us -> none
    pallas_call x1, Pallas kernels: 175 us -> 168 us  [shards(): pl.pallas_call(kernel, out_shape=(jax.ShapeDtypeStruct((OWN, DW), bf), ja...]
    pallas_call x0 -> x1, Pallas kernels: none -> 4.81 us  [shards(): pl.pallas_call(hand_over, out_shape=tuple((jax.ShapeDtypeStruct(r.shape,...]
where the time goes in v3:
time: 174 us
  Pallas kernels  173 us (99%)
    pallas_call x1, Pallas kernels, shards(): pl.pallas_call(kernel, out_shape=(jax.ShapeDtypeStruct((OWN, DW), bf), ja...  168 us
    pallas_call x1, Pallas kernels, shards(): pl.pallas_call(hand_over, out_shape=tuple((jax.ShapeDtypeStruct(r.shape,...  4.81 us

profile of v3, /device:TPU:0, one launch (start us, length us, event | category | flops | bytes accessed | tf_op | source)
XLA Modules:
  0.0 173.7 jit_solution(6159125789955804941)
XLA Ops:
  0.6 168.3 %sparse_ffn.1 = (bf16[48,1536]{1,0:T(8,128)(2,1)}, bf16[48,1536]{1,0:T(8,128)(2,1)}, bf16[12,6,128,128]{3,2,1,0:T(8,128)(2,1)}, bf16[24,3,128,128]{3,2,1,0:T(8,128)(2,1)}) custom-call(s32[6,12]{1,0:T(8,128)} %bitcast.6, s32[3,24]{1,0:T(4,128)} %bitcast.7, bf16[48,1536]{1,0:T(8,128)(2,1)} %x_in.1, bf16[48,1536]{1,0:T(8,128)(2,1)} %c_in.1, ...), custom_call_target="tpu_custom_call" | custom-call | tf_op jit(solution)/shard_map/sparse_ffn/pallas_call | solution.py:602
  168.9 4.8 %hand_over.1 = (bf16[48,1536]{1,0:T(8,128)(2,1)}, bf16[48,1536]{1,0:T(8,128)(2,1)}, bf16[12,6,128,128]{3,2,1,0:T(8,128)(2,1)}, bf16[24,3,128,128]{3,2,1,0:T(8,128)(2,1)}) custom-call(bf16[48,1536]{1,0:T(8,128)(2,1)} %get-tuple-element.8.refs_0_, bf16[48,1536]{1,0:T(8,128)(2,1)} %get-tuple-element.9.refs_1_, ...), custom_call_target="tpu_custom_call" | custom-call | tf_op jit(solution)/shard_map/hand_over/pallas_call | solution.py:655

commit v4 on v3

--- a/solution.py
+++ b/solution.py
@@ -506,9 +506,9 @@
         return find
 
     gathers = [
-        (1, (None, None, 0, 2, 4)),
-        (2, (None, 2, 4, 6, 8)),
-        (3, (1, 4, 7, 9, 12)),
+        (1, (None, None, 0, 2, 3)),
+        (2, (None, 2, 4, 6, 7)),
+        (3, (1, 4, 7, 9, 11)),
         (4, (7, 10, 13, 16, 19)),
         (5, (13, 16, 19, 22, 25)),
     ]
@@ -531,13 +531,13 @@
         run(0, ag_unit, gather1)
         run(S3, rs_unit, stage3)
         run(S2, rs_unit, stage2)
+        run(0, rs_unit, product)
         for step in range(4, -1, -1):
             run(0, at_ticks([(e, ticks[step]) for e, ticks in gathers if ticks[step] is not None]),
                 lambda e, step=step: gather_step(e // NG, e % NG, step))
         for step in range(3, -1, -1):
             run(0, at_ticks([(e, ticks[step]) for e, ticks in scatters if ticks[step] < TICKS]),
                 lambda e, step=step: scatter_step(e // NG, e % NG, step))
-        run(0, rs_unit, product)
         run(A4, ag_unit, use)
 
         @pl.when(t == 28)
@@ -558,12 +558,10 @@
 
     lax.fori_loop(0, TICKS, tick, 0)
     scatter_step(1, NG - 1, 0, direct=True)
-    for e, ticks in scatters:
-        for step in range(4):
-            if ticks[step] >= TICKS:
-                scatter_step(e // NG, e % NG, step)
+    scatter_step(1, NG - 2, 2)
+    scatter_step(1, NG - 1, 1, direct=True)
     first(0)
-    scatter_step(1, NG - 1, 1, direct=True)
+    scatter_step(1, NG - 2, 3)
     for i in range(1, 12):
         first(i)
     scatter_step(1, NG - 1, 3, direct=True)

time: 174 us -> 172 us (0.989)
  no operation moved by 1% of the time
where the time goes in v4:
time: 172 us
  Pallas kernels  172 us (100%)
    pallas_call x1, Pallas kernels, shards(): pl.pallas_call(kernel, out_shape=(jax.ShapeDtypeStruct((OWN, DW), bf), ja...  167 us
    pallas_call x1, Pallas kernels, shards(): pl.pallas_call(hand_over, out_shape=tuple((jax.ShapeDtypeStruct(r.shape,...  4.81 us

profile of v4, /device:TPU:0, one launch (start us, length us, event | category | flops | bytes accessed | tf_op | source)
XLA Modules:
  0.0 172.3 jit_solution(16514896156100588655)
XLA Ops:
  0.6 166.8 %sparse_ffn.1 = (bf16[48,1536]{1,0:T(8,128)(2,1)}, bf16[48,1536]{1,0:T(8,128)(2,1)}, bf16[12,6,128,128]{3,2,1,0:T(8,128)(2,1)}, bf16[24,3,128,128]{3,2,1,0:T(8,128)(2,1)}) custom-call(s32[6,12]{1,0:T(8,128)} %bitcast.6, s32[3,24]{1,0:T(4,128)} %bitcast.7, bf16[48,1536]{1,0:T(8,128)(2,1)} %x_in.1, bf16[48,1536]{1,0:T(8,128)(2,1)} %c_in.1, ...), custom_call_target="tpu_custom_call" | custom-call | tf_op jit(solution)/shard_map/sparse_ffn/pallas_call | solution.py:600
  167.5 4.8 %hand_over.1 = (bf16[48,1536]{1,0:T(8,128)(2,1)}, bf16[48,1536]{1,0:T(8,128)(2,1)}, bf16[12,6,128,128]{3,2,1,0:T(8,128)(2,1)}, bf16[24,3,128,128]{3,2,1,0:T(8,128)(2,1)}) custom-call(bf16[48,1536]{1,0:T(8,128)(2,1)} %get-tuple-element.8.refs_0_, bf16[48,1536]{1,0:T(8,128)(2,1)} %get-tuple-element.9.refs_1_, ...), custom_call_target="tpu_custom_call" | custom-call | tf_op jit(solution)/shard_map/hand_over/pallas_call | solution.py:653

commit v5 on v4

--- a/solution.py
+++ b/solution.py
@@ -206,19 +206,22 @@
         return rs(u, 0, sy_y.at[u % NT], ry_y.at[u % NS], dev_y)
 
     def rs_zo_y(u, d):
-        return rs(u, 1 + d, szo_y.at[u % NT, d], rzo_y.at[u % NS, d], dev_z[d])
+        return rs(u, 1, szo_y.at[u % NT, d], rzo_y.at[u % NS, d], dev_z[d])
 
     def rs_z_y(u, d):
-        return rs(u, 3 + d, sz_y.at[u % NT, d], rz_y.at[u % NS, d], dev_z[d])
+        return rs(u, 2, sz_y.at[u % NT, d], rz_y.at[u % NS, d], dev_z[d])
 
     def rs_zo_z(u, d):
-        return rs(u, 5 + d, szo_z.at[u % NT, d], rzo_z.at[u % NS, d], dev_z[d])
+        return rs(u, 3, szo_z.at[u % NT, d], rzo_z.at[u % NS, d], dev_z[d])
 
     def rs_z_z(u, d):
-        return rs(u, 7 + d, sz_z.at[u % NT, d], rz_z.at[u % NS, d], dev_z[d])
+        return rs(u, 4, sz_z.at[u % NT, d], rz_z.at[u % NS, d], dev_z[d])
 
     def rs_y_z(u):
-        return rs(u, 9, sy_z.at[u % NT], ry_z.at[u % NS], dev_y)
+        return rs(u, 5, sy_z.at[u % NT], ry_z.at[u % NS], dev_y)
+
+    def rs_both(u, k, sent, got):
+        rs(u, k, sent.at[u % NT], got.at[u % NS], dev_z[0]).wait()
 
     def product(u):
         sp, s2 = u % NP, u % NT
@@ -246,8 +249,8 @@
         for d in range(2):
             szo_y[s2, d] = bf16(part[sp, zo, y, :, yh[d]] + f32(ry_y[s, zo, :, yh[d]]))
             rs_zo_y(u, d).start()
-        for d in range(2):
-            rs_zo_z(u, d).wait()
+        rs_both(u, 3, szo_z, rzo_z)
+        for d in range(2):
             for e in range(2):
                 total = part[sp, tgt[d], :, :, zh[e]]
                 if e == d:
@@ -257,24 +260,22 @@
 
     def stage3(u):
         s, sp, s2 = u % NS, u % NP, u % NT
-        for d in range(2):
-            rs_zo_y(u, d).wait()
+        rs_both(u, 1, szo_y, rzo_y)
+        for d in range(2):
             for e in range(2):
                 total = part[sp, tgt[d], y, :, yh[e]] + f32(ry_y[s, tgt[d], :, yh[e]])
                 if e == d:
                     total = total + f32(rzo_y[s, d])
                 sz_y[s2, d, :, yh[e]] = bf16(total)
             rs_z_y(u, d).start()
-        for d in range(2):
-            rs_z_z(u, d).wait()
+        rs_both(u, 4, sz_z, rz_z)
         sy_z[s2] = bf16(part[sp, z, yo, :, zw] + f32(rz_z[s, 0, yo]) + f32(rz_z[s, 1, yo]))
         rs_y_z(u).start()
 
     def stage4(u):
         s, sp = u % NS, u % NP
         g, c = (u // NC) % NG, u % NC
-        for d in range(2):
-            rs_z_y(u, d).wait()
+        rs_both(u, 2, sz_y, rz_y)
         sum_y = part[sp, z, y, :, yw] + f32(ry_y[s, z]) + f32(rz_y[s, 0]) + f32(rz_y[s, 1])
         rs_y_z(u).wait()
         sum_z = part[sp, z, y, :, zw] + f32(rz_z[s, 0, y]) + f32(rz_z[s, 1, y]) + f32(ry_z[s])
@@ -418,11 +419,9 @@
         first_out(i).start()
 
     def scatter_step(p, g, step, direct=False):
-        e = p * NG + g
-
         def rr(k, src, dst, ax, ayl, ac=core):
-            send = rr_s.at[e, 0 if k == 0 else 2 if k == 7 else 1]
-            return copy(src, dst, send, rr_r.at[e, k], (at_row(ax, ayl, ac), col))
+            send = rr_s.at[g, 0 if k == 0 else 2 if k == 7 else 1]
+            return copy(src, dst, send, rr_r.at[g, k], (at_row(ax, ayl, ac), col))
 
         def over_core():
             return rr(0, acc.at[p, g, :, co], rd.at[g], x, yl, co)
@@ -641,8 +640,8 @@
             pltpu.SMEM((12, 24), jnp.int32),
             pltpu.SMEM((24, 12), jnp.int32),
             dma((6,)),
-            dma((NT, 10)), dma((NR, 10)), dma((NT, 10)), dma((NR, 10)),
-            dma((2, NG, 2)), dma((2, NG, 8)), dma((2 * NG, 3)), dma((2 * NG, 8)),
+            dma((NT, 6)), dma((NR, 6)), dma((NT, 10)), dma((NR, 10)),
+            dma((2, NG, 2)), dma((2, NG, 8)), dma((NG, 3)), dma((NG, 8)),
         ],
         compiler_params=pltpu.CompilerParams(
             collective_id=1, has_side_effects=True, vmem_limit_bytes=62 * 2**20

time: 172 us -> 172 us (level)
  no operation moved by 1% of the time
where the time goes in v5:
time: 172 us
  Pallas kernels  171 us (99%)
    pallas_call x1, Pallas kernels, shards(): pl.pallas_call(kernel, out_shape=(jax.ShapeDtypeStruct((OWN, DW), bf), ja...  166 us
    pallas_call x1, Pallas kernels, shards(): pl.pallas_call(hand_over, out_shape=tuple((jax.ShapeDtypeStruct(r.shape,...  4.81 us

profile of v5, /device:TPU:0, one launch (start us, length us, event | category | flops | bytes accessed | tf_op | source)
XLA Modules:
  0.0 171.7 jit_solution(14144584102140343533)
XLA Ops:
  0.6 166.2 %sparse_ffn.1 = (bf16[48,1536]{1,0:T(8,128)(2,1)}, bf16[48,1536]{1,0:T(8,128)(2,1)}, bf16[12,6,128,128]{3,2,1,0:T(8,128)(2,1)}, bf16[24,3,128,128]{3,2,1,0:T(8,128)(2,1)}) custom-call(s32[6,12]{1,0:T(8,128)} %bitcast.6, s32[3,24]{1,0:T(4,128)} %bitcast.7, bf16[48,1536]{1,0:T(8,128)(2,1)} %x_in.1, bf16[48,1536]{1,0:T(8,128)(2,1)} %c_in.1, ...), custom_call_target="tpu_custom_call" | custom-call | tf_op jit(solution)/shard_map/sparse_ffn/pallas_call | solution.py:599
  166.9 4.8 %hand_over.1 = (bf16[48,1536]{1,0:T(8,128)(2,1)}, bf16[48,1536]{1,0:T(8,128)(2,1)}, bf16[12,6,128,128]{3,2,1,0:T(8,128)(2,1)}, bf16[24,3,128,128]{3,2,1,0:T(8,128)(2,1)}) custom-call(bf16[48,1536]{1,0:T(8,128)(2,1)} %get-tuple-element.8.refs_0_, bf16[48,1536]{1,0:T(8,128)(2,1)} %get-tuple-element.9.refs_1_, ...), custom_call_target="tpu_custom_call" | custom-call | tf_op jit(solution)/shard_map/hand_over/pallas_call | solution.py:652
